TPU v7x, 768 devices: a whole 4x8x12 slice. The times are simulated.
768 devices in a mesh: seq: 384 (over z, x, y), head: 2 (over core).
Axes of the slice: x: 4, y: 8, z: 12, core: 2. Of those that a mesh axis runs over, the one named last changes fastest.
Arguments:
- query_raw: bfloat16 [98304, 8, 128], P('seq', 'head'), may hold values from -6 to 6
- key_raw: bfloat16 [98304, 8, 128], P('seq', 'head'), may hold values from -6 to 6
- value_raw: bfloat16 [98304, 8, 128], P('seq', 'head'), may hold values from -6 to 6
- out_gain: float32 [8, 128], P('head'), may hold values from 0.5 to 1.5
- out_grad: bfloat16 [98304, 8, 128], P('seq', 'head'), may hold values from -6 to 6
Outputs:
- normed_out: bfloat16 [98304, 8, 128], P('seq', 'head')
- query_grad: bfloat16 [98304, 8, 128], P('seq', 'head')
- key_grad: bfloat16 [98304, 8, 128], P('seq', 'head')
- value_grad: bfloat16 [98304, 8, 128], P('seq', 'head')
All inputs are finite; a program needn't handle non-finite values.
Results may differ from a plain program's by a relative error of at most 0.0065.
Values sent between devices are 32-bit elements; how exact they have to be, the bound alone decides.
A program may use at most 32 MiB of HBM per device.

v0:
```python
import jax
import jax.numpy as jnp
from jax import lax
from jax.sharding import PartitionSpec as P

GROUP = 256


def from_behind(shard, axis, by):
    count = lax.axis_size(axis)
    pairs = [(i, i + by) for i in range(count) if 0 <= i + by < count]
    return lax.ppermute(shard, axis, pairs)


def silu_grad(raw):
    sigma = jax.nn.sigmoid(raw)
    return sigma * (1.0 + raw * (1.0 - sigma))


def causal_mask(length):
    rows = lax.broadcasted_iota(jnp.int32, (length, length), 0)
    cols = lax.broadcasted_iota(jnp.int32, (length, length), 1)
    return cols <= rows


def lower_sum(own_total):
    inclusive = own_total
    stride = 1
    while stride < lax.axis_size("seq"):
        inclusive = inclusive + from_behind(inclusive, "seq", stride)
        stride = stride * 2
    return inclusive - own_total


def upper_sum(own_total):
    inclusive = own_total
    stride = 1
    while stride < lax.axis_size("seq"):
        inclusive = inclusive + from_behind(inclusive, "seq", -stride)
        stride = stride * 2
    return inclusive - own_total


def body(query_raw, key_raw, value_raw, out_gain, out_grad):
    tok_rows, head_count, width = query_raw.shape
    blocks = tok_rows // GROUP
    blocked = (blocks, GROUP, head_count, width)
    query_act = jax.nn.silu(query_raw.astype(jnp.float32)).astype(jnp.bfloat16).reshape(blocked)
    key_act = jax.nn.silu(key_raw.astype(jnp.float32)).astype(jnp.bfloat16).reshape(blocked)
    value_blk = value_raw.reshape(blocked)
    mask = causal_mask(GROUP)[None, None]
    block_kv = jnp.einsum("cshd,cshe->chde", key_act, value_blk, preferred_element_type=jnp.float32)
    own_total = jnp.sum(block_kv, axis=0)
    before = lower_sum(own_total)
    state_b = (before[None] + (jnp.cumsum(block_kv, axis=0) - block_kv)).astype(jnp.bfloat16)
    scores = jnp.einsum("cthd,cshd->chts", query_act, key_act, preferred_element_type=jnp.float32)
    attn = jnp.where(mask, scores, 0.0).astype(jnp.bfloat16)
    mixed = jnp.einsum("chts,cshe->cthe", attn, value_blk, preferred_element_type=jnp.float32)
    mixed = mixed + jnp.einsum(
        "cthd,chde->cthe", query_act, state_b, preferred_element_type=jnp.float32
    )
    mixed = mixed.reshape(tok_rows, head_count, width)
    grad_in = out_grad.astype(jnp.float32) * out_gain
    sq_part = jnp.sum(mixed * mixed, axis=(1, 2))
    cross_part = jnp.sum(grad_in * mixed, axis=(1, 2))
    sq_total, cross_total = lax.psum((sq_part, cross_part), "head")
    features = head_count * width * lax.axis_size("head")
    inv_rms = lax.rsqrt(sq_total / features + 1e-06)
    normed_out = (mixed * inv_rms[:, None, None] * out_gain).astype(jnp.bfloat16)
    delta = (
        grad_in * inv_rms[:, None, None]
        - mixed * (cross_total * inv_rms**3 / features)[:, None, None]
    ).astype(jnp.bfloat16)
    delta_blk = delta.reshape(blocked)
    block_grad = jnp.einsum(
        "cthd,cthe->chde", query_act, delta_blk, preferred_element_type=jnp.float32
    )
    own_grad = jnp.sum(block_grad, axis=0)
    after = upper_sum(own_grad)
    local_after = jnp.flip(jnp.cumsum(jnp.flip(block_grad, 0), axis=0), 0) - block_grad
    grad_state = (after[None] + local_after).astype(jnp.bfloat16)
    bscore = jnp.einsum("cthe,cshe->chts", delta_blk, value_blk, preferred_element_type=jnp.float32)
    bscore = jnp.where(mask, bscore, 0.0).astype(jnp.bfloat16)
    dquery = jnp.einsum("chts,cshd->cthd", bscore, key_act, preferred_element_type=jnp.float32)
    dquery = dquery + jnp.einsum(
        "cthe,chde->cthd", delta_blk, state_b, preferred_element_type=jnp.float32
    )
    dkey = jnp.einsum("chts,cthd->cshd", bscore, query_act, preferred_element_type=jnp.float32)
    dkey = dkey + jnp.einsum(
        "cshe,chde->cshd", value_blk, grad_state, preferred_element_type=jnp.float32
    )
    dvalue = jnp.einsum("chts,cthe->cshe", attn, delta_blk, preferred_element_type=jnp.float32)
    dvalue = dvalue + jnp.einsum(
        "cshd,chde->cshe", key_act, grad_state, preferred_element_type=jnp.float32
    )
    whole = (tok_rows, head_count, width)
    query_grad = (dquery.reshape(whole) * silu_grad(query_raw.astype(jnp.float32))).astype(
        jnp.bfloat16
    )
    key_grad = (dkey.reshape(whole) * silu_grad(key_raw.astype(jnp.float32))).astype(jnp.bfloat16)
    value_grad = dvalue.reshape(whole).astype(jnp.bfloat16)
    return (normed_out, query_grad, key_grad, value_grad)


def solution(mesh):
    in_specs = (
        P("seq", "head", None),
        P("seq", "head", None),
        P("seq", "head", None),
        P("head", None),
        P("seq", "head", None),
    )
    out_specs = (
        P("seq", "head", None),
        P("seq", "head", None),
        P("seq", "head", None),
        P("seq", "head", None),
    )
    return jax.shard_map(body, mesh=mesh, in_specs=in_specs, out_specs=out_specs, check_vma=False)
```

profile of v0, /device:TPU:126, one launch (start us, length us, event | category | flops | bytes accessed | tf_op | source)
XLA Modules:
  0.0 290.4 jit_solution(7269268948791583722)
XLA Ops:
  0.6 0.0 copy-start
  0.6 1.1 copy.10
  1.8 0.0 copy-done
  1.8 0.3 fusion.26
  2.1 3.4 %collective-permute-start = (f32[4,128,128]{2,1,0:T(8,128)S(1)}, f32[4,128,128]{2,1,0:T(8,128)S(1)}, u32[]{:S(2)}, u32[]{:S(2)}) collective-permute-start(f32[4,128,128]{2,1,0:T(8,128)S(1)} %fusion.26), channel_id=1, source_target_pairs={{0,2},{2,4},{4,6},{6,8},{8,10},{10,12},{12,14},{14,16},{16,18},{18... | collective-permute-start | bytes 786440 | tf_op jit(solution)/shard_map/ppermute | solution.py:12
  5.5 6.5 %collective-permute-done = f32[4,128,128]{2,1,0:T(8,128)S(1)} collective-permute-done((f32[4,128,128]{2,1,0:T(8,128)S(1)}, f32[4,128,128]{2,1,0:T(8,128)S(1)}, u32[]{:S(2)}, u32[]{:S(2)}) %collective-permute-start) | collective-permute-done | bytes 262176 | tf_op jit(solution)/shard_map/ppermute | solution.py:12
  12.1 4.4 %collective-permute-start.1 = (f32[4,128,128]{2,1,0:T(8,128)S(1)}, f32[4,128,128]{2,1,0:T(8,128)S(1)}, u32[]{:S(2)}, u32[]{:S(2)}) collective-permute-start(f32[4,128,128]{2,1,0:T(8,128)S(1)} %add.125), channel_id=1, source_target_pairs={{0,4},{2,6},{4,8},{6,10},{8,12},{10,14},{12,16},{14,18},{16,20},{1... | collective-permute-start | bytes 786440 | tf_op jit(solution)/shard_map/ppermute | solution.py:12
  16.5 13.2 %collective-permute-done.1 = f32[4,128,128]{2,1,0:T(8,128)S(1)} collective-permute-done((f32[4,128,128]{2,1,0:T(8,128)S(1)}, f32[4,128,128]{2,1,0:T(8,128)S(1)}, u32[]{:S(2)}, u32[]{:S(2)}) %collective-permute-start.1) | collective-permute-done | bytes 262176 | tf_op jit(solution)/shard_map/ppermute | solution.py:12
  29.7 1.9 collective-permute-start.2
  31.7 12.8 %collective-permute-done.2 = f32[4,128,128]{2,1,0:T(8,128)S(1)} collective-permute-done((f32[4,128,128]{2,1,0:T(8,128)S(1)}, f32[4,128,128]{2,1,0:T(8,128)S(1)}, u32[]{:S(2)}, u32[]{:S(2)}) %collective-permute-start.2) | collective-permute-done | bytes 262176 | tf_op jit(solution)/shard_map/ppermute | solution.py:12
  44.6 2.3 collective-permute-start.3
  46.8 6.0 %collective-permute-done.3 = f32[4,128,128]{2,1,0:T(8,128)S(1)} collective-permute-done((f32[4,128,128]{2,1,0:T(8,128)S(1)}, f32[4,128,128]{2,1,0:T(8,128)S(1)}, u32[]{:S(2)}, u32[]{:S(2)}) %collective-permute-start.3) | collective-permute-done | bytes 262176 | tf_op jit(solution)/shard_map/ppermute | solution.py:12
  52.9 2.8 collective-permute-start.4
  55.7 7.0 %collective-permute-done.4 = f32[4,128,128]{2,1,0:T(8,128)S(1)} collective-permute-done((f32[4,128,128]{2,1,0:T(8,128)S(1)}, f32[4,128,128]{2,1,0:T(8,128)S(1)}, u32[]{:S(2)}, u32[]{:S(2)}) %collective-permute-start.4) | collective-permute-done | bytes 262176 | tf_op jit(solution)/shard_map/ppermute | solution.py:12
  62.7 4.0 %collective-permute-start.5 = (f32[4,128,128]{2,1,0:T(8,128)S(1)}, f32[4,128,128]{2,1,0:T(8,128)S(1)}, u32[]{:S(2)}, u32[]{:S(2)}) collective-permute-start(f32[4,128,128]{2,1,0:T(8,128)S(1)} %add.129), channel_id=1, source_target_pairs={{0,64},{2,66},{4,68},{6,70},{8,72},{10,74},{12,76},{14,78},{16,80}... | collective-permute-start | bytes 786440 | tf_op jit(solution)/shard_map/ppermute | solution.py:12
  66.7 7.2 %collective-permute-done.5 = f32[4,128,128]{2,1,0:T(8,128)S(1)} collective-permute-done((f32[4,128,128]{2,1,0:T(8,128)S(1)}, f32[4,128,128]{2,1,0:T(8,128)S(1)}, u32[]{:S(2)}, u32[]{:S(2)}) %collective-permute-start.5) | collective-permute-done | bytes 262176 | tf_op jit(solution)/shard_map/ppermute | solution.py:12
  73.9 0.0 copy-start.1
  73.9 3.1 %collective-permute-start.6 = (f32[4,128,128]{2,1,0:T(8,128)S(1)}, f32[4,128,128]{2,1,0:T(8,128)S(1)}, u32[]{:S(2)}, u32[]{:S(2)}) collective-permute-start(f32[4,128,128]{2,1,0:T(8,128)S(1)} %add.130), channel_id=1, source_target_pairs={{0,128},{2,130},{4,132},{6,134},{8,136},{10,138},{12,140},{14,142}... | collective-permute-start | bytes 786440 | tf_op jit(solution)/shard_map/ppermute | solution.py:12
  77.0 6.7 %collective-permute-done.6 = f32[4,128,128]{2,1,0:T(8,128)S(1)} collective-permute-done((f32[4,128,128]{2,1,0:T(8,128)S(1)}, f32[4,128,128]{2,1,0:T(8,128)S(1)}, u32[]{:S(2)}, u32[]{:S(2)}) %collective-permute-start.6) | collective-permute-done | bytes 262176 | tf_op jit(solution)/shard_map/ppermute | solution.py:12
  83.8 28.0 %collective-permute-start.7 = (f32[4,128,128]{2,1,0:T(8,128)S(1)}, f32[4,128,128]{2,1,0:T(8,128)S(1)}, u32[]{:S(2)}, u32[]{:S(2)}) collective-permute-start(f32[4,128,128]{2,1,0:T(8,128)S(1)} %add.131), channel_id=1, source_target_pairs={{0,256},{2,258},{4,260},{6,262},{8,264},{10,266},{12,268},{14,270}... | collective-permute-start | bytes 786440 | tf_op jit(solution)/shard_map/ppermute | solution.py:12
  111.8 0.2 copy.9
  112.0 3.7 %collective-permute-done.7 = f32[4,128,128]{2,1,0:T(8,128)S(1)} collective-permute-done((f32[4,128,128]{2,1,0:T(8,128)S(1)}, f32[4,128,128]{2,1,0:T(8,128)S(1)}, u32[]{:S(2)}, u32[]{:S(2)}) %collective-permute-start.7) | collective-permute-done | bytes 262176 | tf_op jit(solution)/shard_map/ppermute | solution.py:12
  115.8 0.0 copy-start.2
  115.8 11.1 %collective-permute-start.8 = (f32[4,128,128]{2,1,0:T(8,128)S(1)}, f32[4,128,128]{2,1,0:T(8,128)S(1)}, u32[]{:S(2)}, u32[]{:S(2)}) collective-permute-start(f32[4,128,128]{2,1,0:T(8,128)S(1)} %add.132), channel_id=1, source_target_pairs={{0,512},{2,514},{4,516},{6,518},{8,520},{10,522},{12,524},{14,526}... | collective-permute-start | bytes 786440 | tf_op jit(solution)/shard_map/ppermute | solution.py:12
  126.8 0.5 fusion
  127.3 0.0 copy-done.2
  127.3 0.2 copy.17
  127.5 0.3 convolution_bitcast_fusion
  127.8 0.0 copy-start.3
  127.9 2.8 collective-permute-done.8
  130.7 0.3 multiply_reduce_fusion
  131.1 2.5 all-reduce
  133.6 0.2 subtract_convert_fusion
  133.7 0.3 fusion.35
  134.0 5.2 %collective-permute-start.9 = (f32[4,128,128]{2,1,0:T(8,128)S(1)}, f32[4,128,128]{2,1,0:T(8,128)S(1)}, u32[]{:S(2)}, u32[]{:S(2)}) collective-permute-start(f32[4,128,128]{2,1,0:T(8,128)S(1)} %fusion.35), channel_id=1, source_target_pairs={{2,0},{4,2},{6,4},{8,6},{10,8},{12,10},{14,12},{16,14},{18,16},{20... | collective-permute-start | bytes 786440 | tf_op jit(solution)/shard_map/ppermute | solution.py:12
  139.3 13.4 %collective-permute-done.9 = f32[4,128,128]{2,1,0:T(8,128)S(1)} collective-permute-done((f32[4,128,128]{2,1,0:T(8,128)S(1)}, f32[4,128,128]{2,1,0:T(8,128)S(1)}, u32[]{:S(2)}, u32[]{:S(2)}) %collective-permute-start.9) | collective-permute-done | bytes 262176 | tf_op jit(solution)/shard_map/ppermute | solution.py:12
  152.7 1.9 collective-permute-start.10
  154.6 15.3 %collective-permute-done.10 = f32[4,128,128]{2,1,0:T(8,128)S(1)} collective-permute-done((f32[4,128,128]{2,1,0:T(8,128)S(1)}, f32[4,128,128]{2,1,0:T(8,128)S(1)}, u32[]{:S(2)}, u32[]{:S(2)}) %collective-permute-start.10) | collective-permute-done | bytes 262176 | tf_op jit(solution)/shard_map/ppermute | solution.py:12
  170.0 2.0 collective-permute-start.11
  171.9 15.9 %collective-permute-done.11 = f32[4,128,128]{2,1,0:T(8,128)S(1)} collective-permute-done((f32[4,128,128]{2,1,0:T(8,128)S(1)}, f32[4,128,128]{2,1,0:T(8,128)S(1)}, u32[]{:S(2)}, u32[]{:S(2)}) %collective-permute-start.11) | collective-permute-done | bytes 262176 | tf_op jit(solution)/shard_map/ppermute | solution.py:12
  187.9 1.9 collective-permute-start.12
  189.8 8.6 %collective-permute-done.12 = f32[4,128,128]{2,1,0:T(8,128)S(1)} collective-permute-done((f32[4,128,128]{2,1,0:T(8,128)S(1)}, f32[4,128,128]{2,1,0:T(8,128)S(1)}, u32[]{:S(2)}, u32[]{:S(2)}) %collective-permute-start.12) | collective-permute-done | bytes 262176 | tf_op jit(solution)/shard_map/ppermute | solution.py:12
  198.4 5.0 %collective-permute-start.13 = (f32[4,128,128]{2,1,0:T(8,128)S(1)}, f32[4,128,128]{2,1,0:T(8,128)S(1)}, u32[]{:S(2)}, u32[]{:S(2)}) collective-permute-start(f32[4,128,128]{2,1,0:T(8,128)S(1)} %add.147), channel_id=1, source_target_pairs={{32,0},{34,2},{36,4},{38,6},{40,8},{42,10},{44,12},{46,14},{48,16}... | collective-permute-start | bytes 786440 | tf_op jit(solution)/shard_map/ppermute | solution.py:12
  203.5 5.6 %collective-permute-done.13 = f32[4,128,128]{2,1,0:T(8,128)S(1)} collective-permute-done((f32[4,128,128]{2,1,0:T(8,128)S(1)}, f32[4,128,128]{2,1,0:T(8,128)S(1)}, u32[]{:S(2)}, u32[]{:S(2)}) %collective-permute-start.13) | collective-permute-done | bytes 262176 | tf_op jit(solution)/shard_map/ppermute | solution.py:12
  209.1 8.7 %collective-permute-start.14 = (f32[4,128,128]{2,1,0:T(8,128)S(1)}, f32[4,128,128]{2,1,0:T(8,128)S(1)}, u32[]{:S(2)}, u32[]{:S(2)}) collective-permute-start(f32[4,128,128]{2,1,0:T(8,128)S(1)} %add.148), channel_id=1, source_target_pairs={{64,0},{66,2},{68,4},{70,6},{72,8},{74,10},{76,12},{78,14},{80,16}... | collective-permute-start | bytes 786440 | tf_op jit(solution)/shard_map/ppermute | solution.py:12
  217.8 5.7 %collective-permute-done.14 = f32[4,128,128]{2,1,0:T(8,128)S(1)} collective-permute-done((f32[4,128,128]{2,1,0:T(8,128)S(1)}, f32[4,128,128]{2,1,0:T(8,128)S(1)}, u32[]{:S(2)}, u32[]{:S(2)}) %collective-permute-start.14) | collective-permute-done | bytes 262176 | tf_op jit(solution)/shard_map/ppermute | solution.py:12
  223.5 1.3 collective-permute-start.15
  224.8 0.3 fusion.1
  225.2 0.0 copy-start.4
  225.2 11.0 %collective-permute-done.15 = f32[4,128,128]{2,1,0:T(8,128)S(1)} collective-permute-done((f32[4,128,128]{2,1,0:T(8,128)S(1)}, f32[4,128,128]{2,1,0:T(8,128)S(1)}, u32[]{:S(2)}, u32[]{:S(2)}) %collective-permute-start.15) | collective-permute-done | bytes 262176 | tf_op jit(solution)/shard_map/ppermute | solution.py:12
  236.2 1.3 collective-permute-start.16
  237.5 0.3 fusion.31
  237.9 0.3 fusion.7
  238.2 37.5 %collective-permute-done.16 = f32[4,128,128]{2,1,0:T(8,128)S(1)} collective-permute-done((f32[4,128,128]{2,1,0:T(8,128)S(1)}, f32[4,128,128]{2,1,0:T(8,128)S(1)}, u32[]{:S(2)}, u32[]{:S(2)}) %collective-permute-start.16) | collective-permute-done | bytes 262176 | tf_op jit(solution)/shard_map/ppermute | solution.py:12
  275.7 1.3 collective-permute-start.17
  277.0 0.2 fusion.41
  277.3 0.9 copy.25
  278.2 0.9 copy.26
  279.0 0.3 fusion.37
  279.3 8.6 %collective-permute-done.17 = f32[4,128,128]{2,1,0:T(8,128)S(1)} collective-permute-done((f32[4,128,128]{2,1,0:T(8,128)S(1)}, f32[4,128,128]{2,1,0:T(8,128)S(1)}, u32[]{:S(2)}, u32[]{:S(2)}) %collective-permute-start.17) | collective-permute-done | bytes 262176 | tf_op jit(solution)/shard_map/ppermute | solution.py:12
  288.0 0.3 fusion.10
  288.3 0.9 copy.28
  289.2 0.3 fusion.8
  289.5 0.9 copy.27
  (25 shorter events, 0.8 us)
Async XLA Ops:
  0.6 1.2 copy-start
  2.1 9.9 %collective-permute-start = (f32[4,128,128]{2,1,0:T(8,128)S(1)}, f32[4,128,128]{2,1,0:T(8,128)S(1)}, u32[]{:S(2)}, u32[]{:S(2)}) collective-permute-start(f32[4,128,128]{2,1,0:T(8,128)S(1)} %fusion.26), channel_id=1, source_target_pairs={{0,2},{2,4},{4,6},{6,8},{8,10},{10,12},{12,14},{14,16},{16,18},{18... | collective-permute-start | bytes 786440 | tf_op jit(solution)/shard_map/ppermute | solution.py:12
  12.1 17.6 %collective-permute-start.1 = (f32[4,128,128]{2,1,0:T(8,128)S(1)}, f32[4,128,128]{2,1,0:T(8,128)S(1)}, u32[]{:S(2)}, u32[]{:S(2)}) collective-permute-start(f32[4,128,128]{2,1,0:T(8,128)S(1)} %add.125), channel_id=1, source_target_pairs={{0,4},{2,6},{4,8},{6,10},{8,12},{10,14},{12,16},{14,18},{16,20},{1... | collective-permute-start | bytes 786440 | tf_op jit(solution)/shard_map/ppermute | solution.py:12
  29.7 14.8 %collective-permute-start.2 = (f32[4,128,128]{2,1,0:T(8,128)S(1)}, f32[4,128,128]{2,1,0:T(8,128)S(1)}, u32[]{:S(2)}, u32[]{:S(2)}) collective-permute-start(f32[4,128,128]{2,1,0:T(8,128)S(1)} %add.126), channel_id=1, source_target_pairs={{0,8},{2,10},{4,12},{6,14},{8,16},{10,18},{12,20},{14,22},{16,24},... | collective-permute-start | bytes 786440 | tf_op jit(solution)/shard_map/ppermute | solution.py:12
  44.6 8.3 %collective-permute-start.3 = (f32[4,128,128]{2,1,0:T(8,128)S(1)}, f32[4,128,128]{2,1,0:T(8,128)S(1)}, u32[]{:S(2)}, u32[]{:S(2)}) collective-permute-start(f32[4,128,128]{2,1,0:T(8,128)S(1)} %add.127), channel_id=1, source_target_pairs={{0,16},{2,18},{4,20},{6,22},{8,24},{10,26},{12,28},{14,30},{16,32}... | collective-permute-start | bytes 786440 | tf_op jit(solution)/shard_map/ppermute | solution.py:12
  52.9 9.8 %collective-permute-start.4 = (f32[4,128,128]{2,1,0:T(8,128)S(1)}, f32[4,128,128]{2,1,0:T(8,128)S(1)}, u32[]{:S(2)}, u32[]{:S(2)}) collective-permute-start(f32[4,128,128]{2,1,0:T(8,128)S(1)} %add.128), channel_id=1, source_target_pairs={{0,32},{2,34},{4,36},{6,38},{8,40},{10,42},{12,44},{14,46},{16,48}... | collective-permute-start | bytes 786440 | tf_op jit(solution)/shard_map/ppermute | solution.py:12
  62.7 11.2 %collective-permute-start.5 = (f32[4,128,128]{2,1,0:T(8,128)S(1)}, f32[4,128,128]{2,1,0:T(8,128)S(1)}, u32[]{:S(2)}, u32[]{:S(2)}) collective-permute-start(f32[4,128,128]{2,1,0:T(8,128)S(1)} %add.129), channel_id=1, source_target_pairs={{0,64},{2,66},{4,68},{6,70},{8,72},{10,74},{12,76},{14,78},{16,80}... | collective-permute-start | bytes 786440 | tf_op jit(solution)/shard_map/ppermute | solution.py:12
  73.9 37.9 %copy-start.1 = (bf16[256,4,128]{2,1,0:T(4,128)(2,1)S(1)}, bf16[256,4,128]{2,1,0:T(4,128)(2,1)}, u32[]{:S(2)}) copy-start(bf16[256,4,128]{2,1,0:T(4,128)(2,1)} %param.5) | copy-start | bytes 786436
  73.9 9.8 %collective-permute-start.6 = (f32[4,128,128]{2,1,0:T(8,128)S(1)}, f32[4,128,128]{2,1,0:T(8,128)S(1)}, u32[]{:S(2)}, u32[]{:S(2)}) collective-permute-start(f32[4,128,128]{2,1,0:T(8,128)S(1)} %add.130), channel_id=1, source_target_pairs={{0,128},{2,130},{4,132},{6,134},{8,136},{10,138},{12,140},{14,142}... | collective-permute-start | bytes 786440 | tf_op jit(solution)/shard_map/ppermute | solution.py:12
  83.8 31.9 %collective-permute-start.7 = (f32[4,128,128]{2,1,0:T(8,128)S(1)}, f32[4,128,128]{2,1,0:T(8,128)S(1)}, u32[]{:S(2)}, u32[]{:S(2)}) collective-permute-start(f32[4,128,128]{2,1,0:T(8,128)S(1)} %add.131), channel_id=1, source_target_pairs={{0,256},{2,258},{4,260},{6,262},{8,264},{10,266},{12,268},{14,270}... | collective-permute-start | bytes 786440 | tf_op jit(solution)/shard_map/ppermute | solution.py:12
  115.8 11.6 %copy-start.2 = (bf16[256,4,128]{2,1,0:T(4,128)(2,1)S(1)}, bf16[256,4,128]{2,1,0:T(4,128)(2,1)}, u32[]{:S(2)}) copy-start(bf16[256,4,128]{2,1,0:T(4,128)(2,1)} %param.9) | copy-start | bytes 786436
  115.8 14.9 %collective-permute-start.8 = (f32[4,128,128]{2,1,0:T(8,128)S(1)}, f32[4,128,128]{2,1,0:T(8,128)S(1)}, u32[]{:S(2)}, u32[]{:S(2)}) collective-permute-start(f32[4,128,128]{2,1,0:T(8,128)S(1)} %add.132), channel_id=1, source_target_pairs={{0,512},{2,514},{4,516},{6,518},{8,520},{10,522},{12,524},{14,526}... | collective-permute-start | bytes 786440 | tf_op jit(solution)/shard_map/ppermute | solution.py:12
  127.8 2.9 copy-start.3
  134.0 18.6 %collective-permute-start.9 = (f32[4,128,128]{2,1,0:T(8,128)S(1)}, f32[4,128,128]{2,1,0:T(8,128)S(1)}, u32[]{:S(2)}, u32[]{:S(2)}) collective-permute-start(f32[4,128,128]{2,1,0:T(8,128)S(1)} %fusion.35), channel_id=1, source_target_pairs={{2,0},{4,2},{6,4},{8,6},{10,8},{12,10},{14,12},{16,14},{18,16},{20... | collective-permute-start | bytes 786440 | tf_op jit(solution)/shard_map/ppermute | solution.py:12
  152.7 17.2 %collective-permute-start.10 = (f32[4,128,128]{2,1,0:T(8,128)S(1)}, f32[4,128,128]{2,1,0:T(8,128)S(1)}, u32[]{:S(2)}, u32[]{:S(2)}) collective-permute-start(f32[4,128,128]{2,1,0:T(8,128)S(1)} %add.144), channel_id=1, source_target_pairs={{4,0},{6,2},{8,4},{10,6},{12,8},{14,10},{16,12},{18,14},{20,16},{2... | collective-permute-start | bytes 786440 | tf_op jit(solution)/shard_map/ppermute | solution.py:12
  170.0 17.9 %collective-permute-start.11 = (f32[4,128,128]{2,1,0:T(8,128)S(1)}, f32[4,128,128]{2,1,0:T(8,128)S(1)}, u32[]{:S(2)}, u32[]{:S(2)}) collective-permute-start(f32[4,128,128]{2,1,0:T(8,128)S(1)} %add.145), channel_id=1, source_target_pairs={{8,0},{10,2},{12,4},{14,6},{16,8},{18,10},{20,12},{22,14},{24,16},... | collective-permute-start | bytes 786440 | tf_op jit(solution)/shard_map/ppermute | solution.py:12
  187.9 10.5 %collective-permute-start.12 = (f32[4,128,128]{2,1,0:T(8,128)S(1)}, f32[4,128,128]{2,1,0:T(8,128)S(1)}, u32[]{:S(2)}, u32[]{:S(2)}) collective-permute-start(f32[4,128,128]{2,1,0:T(8,128)S(1)} %add.146), channel_id=1, source_target_pairs={{16,0},{18,2},{20,4},{22,6},{24,8},{26,10},{28,12},{30,14},{32,16}... | collective-permute-start | bytes 786440 | tf_op jit(solution)/shard_map/ppermute | solution.py:12
  198.4 10.7 %collective-permute-start.13 = (f32[4,128,128]{2,1,0:T(8,128)S(1)}, f32[4,128,128]{2,1,0:T(8,128)S(1)}, u32[]{:S(2)}, u32[]{:S(2)}) collective-permute-start(f32[4,128,128]{2,1,0:T(8,128)S(1)} %add.147), channel_id=1, source_target_pairs={{32,0},{34,2},{36,4},{38,6},{40,8},{42,10},{44,12},{46,14},{48,16}... | collective-permute-start | bytes 786440 | tf_op jit(solution)/shard_map/ppermute | solution.py:12
  209.1 14.4 %collective-permute-start.14 = (f32[4,128,128]{2,1,0:T(8,128)S(1)}, f32[4,128,128]{2,1,0:T(8,128)S(1)}, u32[]{:S(2)}, u32[]{:S(2)}) collective-permute-start(f32[4,128,128]{2,1,0:T(8,128)S(1)} %add.148), channel_id=1, source_target_pairs={{64,0},{66,2},{68,4},{70,6},{72,8},{74,10},{76,12},{78,14},{80,16}... | collective-permute-start | bytes 786440 | tf_op jit(solution)/shard_map/ppermute | solution.py:12
  223.5 12.6 %collective-permute-start.15 = (f32[4,128,128]{2,1,0:T(8,128)S(1)}, f32[4,128,128]{2,1,0:T(8,128)S(1)}, u32[]{:S(2)}, u32[]{:S(2)}) collective-permute-start(f32[4,128,128]{2,1,0:T(8,128)S(1)} %add.149), channel_id=1, source_target_pairs={{128,0},{130,2},{132,4},{134,6},{136,8},{138,10},{140,12},{142,14}... | collective-permute-start | bytes 786440 | tf_op jit(solution)/shard_map/ppermute | solution.py:12
  225.2 12.6 %copy-start.4 = (bf16[4,256,256]{2,1,0:T(8,128)(2,1)}, bf16[4,256,256]{2,1,0:T(8,128)(2,1)S(1)}, u32[]{:S(2)}) copy-start(bf16[4,256,256]{2,1,0:T(8,128)(2,1)S(1)} %fusion.1) | copy-start | bytes 1572868
  236.2 39.5 %collective-permute-start.16 = (f32[4,128,128]{2,1,0:T(8,128)S(1)}, f32[4,128,128]{2,1,0:T(8,128)S(1)}, u32[]{:S(2)}, u32[]{:S(2)}) collective-permute-start(f32[4,128,128]{2,1,0:T(8,128)S(1)} %add.150), channel_id=1, source_target_pairs={{256,0},{258,2},{260,4},{262,6},{264,8},{266,10},{268,12},{270,14}... | collective-permute-start | bytes 786440 | tf_op jit(solution)/shard_map/ppermute | solution.py:12
  275.7 12.2 %collective-permute-start.17 = (f32[4,128,128]{2,1,0:T(8,128)S(1)}, f32[4,128,128]{2,1,0:T(8,128)S(1)}, u32[]{:S(2)}, u32[]{:S(2)}) collective-permute-start(f32[4,128,128]{2,1,0:T(8,128)S(1)} %add.151), channel_id=1, source_target_pairs={{512,0},{514,2},{516,4},{518,6},{520,8},{522,10},{524,12},{526,14}... | collective-permute-start | bytes 786440 | tf_op jit(solution)/shard_map/ppermute | solution.py:12
  277.3 1.7 copy-start.5
where the time goes:
time: 291 us; the launch traced here: 290 us
  waiting for transfers between devices  188 us (65%)
  starting transfers between devices  89.6 us (31%)
  local copies, waits for them, and re-layouts  5 us (2%)
  matrix products  3.8 us (1%)
    ppermute x18, waiting for transfers between devices, from_behind(): return lax.ppermute(shard, axis, pairs)  188 us
    ppermute x18, starting transfers between devices, from_behind(): return lax.ppermute(shard, axis, pairs)  89.6 us
  transfers between devices with their start and end apart: 18, of which 18 were waited for; matrix products, arithmetic and copies ran while one was open for 2% of the time, Pallas kernels for 0%

commit v1 on v0

v1 whole, which is shorter than its diff:
```python
import functools

import jax
import jax.numpy as jnp
from jax import lax
from jax.experimental import pallas as pl
from jax.experimental.pallas import tpu as pltpu
from jax.sharding import PartitionSpec as P

GROUP = 256
DH = 128
PLANE = 32
CHUNKS = 1
MESH = pl.DeviceIdType.MESH
F32 = jnp.float32
BF16 = jnp.bfloat16


def dot(lhs, rhs, contract):
    return lax.dot_general(lhs, rhs, (contract, ((), ())), preferred_element_type=F32)


def nn(lhs, rhs):
    return dot(lhs, rhs, ((1,), (0,)))


def nt(lhs, rhs):
    return dot(lhs, rhs, ((1,), (1,)))


def tn(lhs, rhs):
    return dot(lhs, rhs, ((0,), (0,)))


def kernel(
    levels,
    heads,
    cores,
    q_hbm,
    k_hbm,
    v_hbm,
    gain_ref,
    g_hbm,
    normed_hbm,
    qg_hbm,
    kg_hbm,
    vg_hbm,
    raw,
    out_buf,
    qact,
    kact,
    vact,
    qslope,
    kslope,
    grad_in,
    attn,
    mixed,
    delta,
    dk,
    dv,
    state_b,
    own,
    gathered,
    prefix,
    total,
    z_slots,
    state,
    stats,
    in_sem,
    out_sem,
    send_sem,
    recv_sem,
    z_send_sem,
    z_recv_sem,
    stat_sem,
):
    seq = lax.axis_index("seq")
    core = lax.axis_index("head")
    level = seq // PLANE
    place = lax.rem(seq, PLANE)
    rows = heads * DH // (CHUNKS * PLANE)
    span = heads * DH // CHUNKS
    per = heads // CHUNKS
    width = GROUP // heads

    def plane_peer(step):
        return lax.rem(place + step, PLANE)

    barrier = pltpu.get_barrier_semaphore()

    def greet_plane(step, carry):
        pl.semaphore_signal(
            barrier, inc=1, device_id=(level * PLANE + plane_peer(step), core), device_id_type=MESH
        )
        return carry

    def greet_level(step, carry):
        other = lax.rem(level + step, levels)
        pl.semaphore_signal(
            barrier, inc=1, device_id=(other * PLANE + place, core), device_id_type=MESH
        )
        return carry

    loads = [
        pltpu.make_async_copy(hbm, raw.at[i], in_sem.at[i])
        for i, hbm in enumerate((k_hbm, v_hbm, q_hbm, g_hbm))
    ]
    for load in loads:
        load.start()
    lax.fori_loop(1, PLANE, greet_plane, 0)
    lax.fori_loop(1, levels, greet_level, 0)
    pl.semaphore_signal(barrier, inc=1, device_id=(seq, 1 - core), device_id_type=MESH)

    row = lax.broadcasted_iota(jnp.int32, (GROUP, GROUP), 0)
    col = lax.broadcasted_iota(jnp.int32, (GROUP, GROUP), 1)
    causal = col <= row
    sort = jnp.where(col == lax.rem(row, width) * heads + row // width, 1.0, 0.0).astype(BF16)
    unsort = jnp.where(col == lax.rem(row, heads) * width + row // heads, 1.0, 0.0).astype(BF16)

    def sorted_tiles(i):
        for tile in range(heads):
            yield tile, nn(sort, raw[i, pl.ds(tile * GROUP, GROUP), :])

    def put(dst, tile, value):
        for h in range(heads):
            dst[h, pl.ds(tile * width, width), :] = value[h * width : (h + 1) * width].astype(
                dst.dtype
            )

    def activate(i, act, slope):
        for tile, value in sorted_tiles(i):
            sigma = jax.nn.sigmoid(value)
            put(act, tile, value * sigma)
            put(slope, tile, sigma * (1.0 + value * (1.0 - sigma)))

    def store(i, hbm, head_value):
        values = [head_value(h).astype(BF16) for h in range(heads)]
        for tile in range(heads):
            piece = jnp.concatenate(
                [value[tile * width : (tile + 1) * width] for value in values], axis=0
            )
            out_buf[i, pl.ds(tile * GROUP, GROUP), :] = nn(unsort, piece).astype(BF16)
        copy = pltpu.make_async_copy(out_buf.at[i], hbm, out_sem.at[i])
        copy.start()
        return copy

    def bytes_of(ref, sem):
        return pltpu.make_async_copy(ref, ref, sem)

    others = pl.ds(0, PLANE - 1)

    def scatter(scan, chunk):
        def send(step, carry):
            peer = plane_peer(step)
            pltpu.make_async_remote_copy(
                src_ref=own.at[scan, pl.ds(chunk * span + peer * rows, rows), :],
                dst_ref=gathered.at[scan, chunk, place],
                send_sem=send_sem.at[scan, 0, chunk],
                recv_sem=recv_sem.at[scan, 0, chunk],
                device_id=(level * PLANE + peer, core),
                device_id_type=MESH,
            ).start()
            return carry

        lax.fori_loop(1, PLANE, send, 0)
        gathered[scan, chunk, place] = own[scan, pl.ds(chunk * span + place * rows, rows), :]

    def wait_scatter(scan, chunk):
        bytes_of(gathered.at[scan, chunk, others], recv_sem.at[scan, 0, chunk]).wait()

    def wait_scatter_send(scan, chunk):
        bytes_of(gathered.at[scan, chunk, others], send_sem.at[scan, 0, chunk]).wait()

    def follows(scan, step):
        other = level + step if scan == 0 else level - step
        return (other < levels) if scan == 0 else (other >= 0), other

    def z_copy(scan, chunk, target):
        return pltpu.make_async_remote_copy(
            src_ref=total.at[scan, chunk],
            dst_ref=z_slots.at[scan, chunk, level],
            send_sem=z_send_sem.at[scan, chunk, target],
            recv_sem=z_recv_sem.at[scan, chunk, level],
            device_id=(target * PLANE + place, core),
            device_id_type=MESH,
        )

    def own_prefix(scan, chunk):
        acc = jnp.zeros((rows, DH), F32)
        order = range(PLANE) if scan == 0 else range(PLANE - 1, -1, -1)
        for p in order:
            prefix[scan, chunk, p] = acc
            acc = acc + gathered[scan, chunk, p]
        total[scan, chunk] = acc
        for step in range(1, levels):
            needed, other = follows(scan, step)

            @pl.when(needed)
            def _():
                z_copy(scan, chunk, other).start()

    def level_prefix(scan, chunk):
        z_slots[scan, chunk, level] = jnp.zeros((rows, DH), F32)
        for source in range(levels):
            earlier = source < level if scan == 0 else source > level

            @pl.when(earlier)
            def _():
                bytes_of(
                    z_slots.at[scan, chunk, source], z_recv_sem.at[scan, chunk, source]
                ).wait()

            @pl.when(jnp.logical_not(earlier))
            def _():
                z_slots[scan, chunk, source] = jnp.zeros((rows, DH), F32)

        acc = jnp.zeros((rows, DH), F32)
        for source in range(levels):
            acc = acc + z_slots[scan, chunk, source]
        for p in range(PLANE):
            prefix[scan, chunk, p] = prefix[scan, chunk, p] + acc

    def give_back(scan, chunk):
        def send(step, carry):
            peer = plane_peer(step)
            pltpu.make_async_remote_copy(
                src_ref=prefix.at[scan, chunk, peer],
                dst_ref=state.at[scan, chunk, place],
                send_sem=send_sem.at[scan, 1, chunk],
                recv_sem=recv_sem.at[scan, 1, chunk],
                device_id=(level * PLANE + peer, core),
                device_id_type=MESH,
            ).start()
            return carry

        lax.fori_loop(1, PLANE, send, 0)
        state[scan, chunk, place] = prefix[scan, chunk, place]

    def wait_back(scan, chunk):
        bytes_of(state.at[scan, chunk, others], recv_sem.at[scan, 1, chunk]).wait()

    def drain(scan):
        for chunk in range(CHUNKS):
            wait_scatter_send(scan, chunk)
            bytes_of(state.at[scan, chunk, others], send_sem.at[scan, 1, chunk]).wait()
            for step in range(1, levels):
                needed, other = follows(scan, step)

                @pl.when(needed)
                def _():
                    z_copy(scan, chunk, other).wait_send()

    def middle(scan):
        for chunk in range(CHUNKS):
            wait_scatter(scan, chunk)
            own_prefix(scan, chunk)
        for chunk in range(CHUNKS):
            level_prefix(scan, chunk)
            give_back(scan, chunk)

    def scanned(scan, h):
        chunk, at = h // per, h % per
        parts = PLANE // per
        return state[scan, chunk, pl.ds(at * parts, parts)].reshape(DH, DH).astype(BF16)

    loads[0].wait()
    activate(0, kact, kslope)
    loads[1].wait()
    for tile, value in sorted_tiles(1):
        put(vact, tile, value)
    for h in range(heads):
        own[0, pl.ds(h * DH, DH), :] = tn(kact[h], vact[h])

    pl.semaphore_wait(barrier, PLANE - 1 + levels - 1 + 1)
    for chunk in range(CHUNKS):
        scatter(0, chunk)

    loads[2].wait()
    activate(2, qact, qslope)
    loads[3].wait()
    for tile, value in sorted_tiles(3):
        for h in range(heads):
            grad_in[h, pl.ds(tile * width, width), :] = (
                value[h * width : (h + 1) * width] * gain_ref[pl.ds(h, 1), :]
            )
    for h in range(heads):
        scores = nt(qact[h], kact[h])
        attn[h] = jnp.where(causal, scores, 0.0).astype(BF16)
        mixed[h] = nn(attn[h], vact[h])

    middle(0)
    for chunk in range(CHUNKS):
        wait_back(0, chunk)

    square = jnp.zeros((GROUP, DH), F32)
    crossed = jnp.zeros((GROUP, DH), F32)
    for h in range(heads):
        state_b[h] = scanned(0, h)
        value = mixed[h] + nn(qact[h], state_b[h])
        mixed[h] = value
        square = square + value * value
        crossed = crossed + grad_in[h] * value
    square = jnp.sum(square, axis=1, keepdims=True)
    crossed = jnp.sum(crossed, axis=1, keepdims=True)
    lane = lax.broadcasted_iota(jnp.int32, (GROUP, DH), 1)
    stats[0] = jnp.where(lane == 0, square, jnp.where(lane == 1, crossed, 0.0))
    exchange = pltpu.make_async_remote_copy(
        src_ref=stats.at[0],
        dst_ref=stats.at[1],
        send_sem=stat_sem.at[0],
        recv_sem=stat_sem.at[1],
        device_id=(seq, 1 - core),
        device_id_type=MESH,
    )
    exchange.start()
    exchange.wait_recv()
    both = stats[1]
    features = heads * cores * DH
    square = square + both[:, 0:1]
    crossed = crossed + both[:, 1:2]
    inv_rms = lax.rsqrt(square * (1.0 / features) + 1e-06)
    factor = crossed * (inv_rms * inv_rms * inv_rms) * (1.0 / features)
    for h in range(heads):
        delta[h] = (grad_in[h] * inv_rms - mixed[h] * factor).astype(BF16)
        own[1, pl.ds(h * DH, DH), :] = tn(qact[h], delta[h])
        if (h + 1) % per == 0:
            scatter(1, h // per)

    copies = [
        store(0, normed_hbm, lambda h: mixed[h] * inv_rms * gain_ref[pl.ds(h, 1), :])
    ]
    for h in range(heads):
        bscore = jnp.where(causal, nt(delta[h], vact[h]), 0.0).astype(BF16)
        mixed[h] = (nn(bscore, kact[h]) + nt(delta[h], state_b[h])) * qslope[h]
        dk[h] = tn(bscore, qact[h])
        dv[h] = tn(attn[h], delta[h])
    copies.append(store(1, qg_hbm, lambda h: mixed[h]))
    exchange.wait_send()
    drain(0)

    middle(1)
    for chunk in range(CHUNKS):
        wait_back(1, chunk)
    for h in range(heads):
        state_b[h] = scanned(1, h)
    copies.append(store(2, kg_hbm, lambda h: (dk[h] + nt(vact[h], state_b[h])) * kslope[h]))
    copies.append(store(3, vg_hbm, lambda h: dv[h] + nn(kact[h], state_b[h])))
    drain(1)
    for copy in copies:
        copy.wait()


def body(query_raw, key_raw, value_raw, out_gain, out_grad):
    tokens, heads, width = query_raw.shape
    levels = lax.axis_size("seq") // PLANE
    cores = lax.axis_size("head")
    flat = (tokens * heads, width)
    rows = heads * DH // (CHUNKS * PLANE)
    anywhere = pl.BlockSpec(memory_space=pl.ANY)
    in_vmem = pl.BlockSpec(memory_space=pltpu.VMEM)
    per_head = (heads, GROUP, DH)
    dma = pltpu.SemaphoreType.DMA
    outs = pl.pallas_call(
        functools.partial(kernel, levels, heads, cores),
        out_shape=[jax.ShapeDtypeStruct(flat, BF16)] * 4,
        in_specs=[anywhere, anywhere, anywhere, in_vmem, anywhere],
        out_specs=[anywhere] * 4,
        scratch_shapes=[
            pltpu.VMEM((4,) + flat, BF16),
            pltpu.VMEM((4,) + flat, BF16),
            pltpu.VMEM(per_head, BF16),
            pltpu.VMEM(per_head, BF16),
            pltpu.VMEM(per_head, BF16),
            pltpu.VMEM(per_head, F32),
            pltpu.VMEM(per_head, F32),
            pltpu.VMEM(per_head, F32),
            pltpu.VMEM((heads, GROUP, GROUP), BF16),
            pltpu.VMEM(per_head, F32),
            pltpu.VMEM(per_head, BF16),
            pltpu.VMEM(per_head, F32),
            pltpu.VMEM(per_head, F32),
            pltpu.VMEM((heads, DH, DH), BF16),
            pltpu.VMEM((2, heads * DH, DH), F32),
            pltpu.VMEM((2, CHUNKS, PLANE, rows, DH), F32),
            pltpu.VMEM((2, CHUNKS, PLANE, rows, DH), F32),
            pltpu.VMEM((2, CHUNKS, rows, DH), F32),
            pltpu.VMEM((2, CHUNKS, levels, rows, DH), F32),
            pltpu.VMEM((2, CHUNKS, PLANE, rows, DH), F32),
            pltpu.VMEM((2, GROUP, DH), F32),
            dma((4,)),
            dma((4,)),
            dma((2, 2, CHUNKS)),
            dma((2, 2, CHUNKS)),
            dma((2, CHUNKS, levels)),
            dma((2, CHUNKS, levels)),
            dma((2,)),
        ],
        compiler_params=pltpu.CompilerParams(
            collective_id=0, has_side_effects=True, vmem_limit_bytes=60 * 1024 * 1024
        ),
    )(
        query_raw.reshape(flat),
        key_raw.reshape(flat),
        value_raw.reshape(flat),
        out_gain,
        out_grad.reshape(flat),
    )
    return tuple(out.reshape(tokens, heads, width) for out in outs)


def solution(mesh):
    rows = P("seq", "head", None)
    return jax.shard_map(
        body,
        mesh=mesh,
        in_specs=(rows, rows, rows, P("head", None), rows),
        out_specs=(rows,) * 4,
        check_vma=False,
    )
```

time: 291 us -> 76.8 us (0.26)
  the two profiles are of different devices: /device:TPU:126 before, /device:TPU:1 now
where the time goes in v1:
time: 76.8 us; the launch traced here: 76.5 us
  Pallas kernels  71.3 us (93%)
  local copies, waits for them, and re-layouts  4.58 us (6%)
    pallas_call x1, Pallas kernels, body(): pl.pallas_call(functools.partial(kernel, levels, heads, cores), out_shape...  71.3 us
    unnamed x10, local copies, waits for them, and re-layouts  4.58 us

profile of v1, /device:TPU:1, one launch (start us, length us, event | category | flops | bytes accessed | tf_op | source)
XLA Modules:
  0.0 76.5 jit_solution(5607368666427880118)
XLA Ops:
  0.6 71.3 %shard_map.84 = (bf16[1024,128]{1,0:T(8,128)(2,1)}, bf16[1024,128]{1,0:T(8,128)(2,1)}, bf16[1024,128]{1,0:T(8,128)(2,1)}, bf16[1024,128]{1,0:T(8,128)(2,1)}) custom-call(bf16[1024,128]{1,0:T(8,128)(2,1)} %bitcast.12, bf16[1024,128]{1,0:T(8,128)(2,1)} %bitcast.13, bf16[1024,128]{1,0:T(8,128)(2,1)} %bitcast.14, f32[4,128]{1,0:T(4,128)} %gain_ref.1, ...), custom_call_target="tpu_custom_call" | custom-call | tf_op jit(solution)/shard_map/pallas_call | solution.py:363
  71.9 0.0 copy-start.2
  71.9 1.8 %copy.13 = bf16[256,4,128]{2,1,0:T(4,128)(2,1)} copy(bf16[256,4,128]{2,1,0:T(4,128)(2,1)} %bitcast.11) | data formatting | bytes 524288
  73.7 0.0 copy-done.2
  73.7 0.0 copy-start.1
  73.7 0.7 copy.14
  74.4 0.3 copy-done.1
  74.8 0.0 copy-start
  74.8 0.7 copy.15
  75.5 0.3 copy-done
  75.8 0.7 copy.16
Async XLA Ops:
  71.9 1.8 %copy-start.2 = (bf16[1024,128]{1,0:T(8,128)(2,1)S(1)}, bf16[1024,128]{1,0:T(8,128)(2,1)}, u32[]{:S(2)}) copy-start(bf16[1024,128]{1,0:T(8,128)(2,1)} %get-tuple-element.9) | copy-start | bytes 786436
  73.7 1.0 %copy-start.1 = (bf16[1024,128]{1,0:T(8,128)(2,1)S(1)}, bf16[1024,128]{1,0:T(8,128)(2,1)}, u32[]{:S(2)}) copy-start(bf16[1024,128]{1,0:T(8,128)(2,1)} %get-tuple-element.10) | copy-start | bytes 786436
  74.8 1.0 %copy-start = (bf16[1024,128]{1,0:T(8,128)(2,1)S(1)}, bf16[1024,128]{1,0:T(8,128)(2,1)}, u32[]{:S(2)}) copy-start(bf16[1024,128]{1,0:T(8,128)(2,1)} %get-tuple-element.11) | copy-start | bytes 786436

commit v2 on v1

--- a/solution.py
+++ b/solution.py
@@ -10,7 +10,7 @@
 GROUP = 256
 DH = 128
 PLANE = 32
-CHUNKS = 1
+CHUNKS = 2
 MESH = pl.DeviceIdType.MESH
 F32 = jnp.float32
 BF16 = jnp.bfloat16
@@ -41,12 +41,11 @@
     v_hbm,
     gain_ref,
     g_hbm,
-    normed_hbm,
-    qg_hbm,
-    kg_hbm,
-    vg_hbm,
+    normed_out,
+    qg_out,
+    kg_out,
+    vg_out,
     raw,
-    out_buf,
     qact,
     kact,
     vact,
@@ -67,7 +66,6 @@
     state,
     stats,
     in_sem,
-    out_sem,
     send_sem,
     recv_sem,
     z_send_sem,
@@ -133,16 +131,13 @@
             put(act, tile, value * sigma)
             put(slope, tile, sigma * (1.0 + value * (1.0 - sigma)))
 
-    def store(i, hbm, head_value):
+    def store(out, head_value):
         values = [head_value(h).astype(BF16) for h in range(heads)]
         for tile in range(heads):
             piece = jnp.concatenate(
                 [value[tile * width : (tile + 1) * width] for value in values], axis=0
             )
-            out_buf[i, pl.ds(tile * GROUP, GROUP), :] = nn(unsort, piece).astype(BF16)
-        copy = pltpu.make_async_copy(out_buf.at[i], hbm, out_sem.at[i])
-        copy.start()
-        return copy
+            out[pl.ds(tile * GROUP, GROUP), :] = nn(unsort, piece).astype(BF16)
 
     def bytes_of(ref, sem):
         return pltpu.make_async_copy(ref, ref, sem)
@@ -250,10 +245,11 @@
                 def _():
                     z_copy(scan, chunk, other).wait_send()
 
-    def middle(scan):
+    def middle(scan, work):
         for chunk in range(CHUNKS):
             wait_scatter(scan, chunk)
             own_prefix(scan, chunk)
+        work()
         for chunk in range(CHUNKS):
             level_prefix(scan, chunk)
             give_back(scan, chunk)
@@ -277,24 +273,26 @@
 
     loads[2].wait()
     activate(2, qact, qslope)
-    loads[3].wait()
-    for tile, value in sorted_tiles(3):
-        for h in range(heads):
-            grad_in[h, pl.ds(tile * width, width), :] = (
-                value[h * width : (h + 1) * width] * gain_ref[pl.ds(h, 1), :]
-            )
     for h in range(heads):
         scores = nt(qact[h], kact[h])
         attn[h] = jnp.where(causal, scores, 0.0).astype(BF16)
         mixed[h] = nn(attn[h], vact[h])
 
-    middle(0)
-    for chunk in range(CHUNKS):
-        wait_back(0, chunk)
+    def weigh_grad():
+        loads[3].wait()
+        for tile, value in sorted_tiles(3):
+            for h in range(heads):
+                grad_in[h, pl.ds(tile * width, width), :] = (
+                    value[h * width : (h + 1) * width] * gain_ref[pl.ds(h, 1), :]
+                )
+
+    middle(0, weigh_grad)
 
     square = jnp.zeros((GROUP, DH), F32)
     crossed = jnp.zeros((GROUP, DH), F32)
     for h in range(heads):
+        if h % per == 0:
+            wait_back(0, h // per)
         state_b[h] = scanned(0, h)
         value = mixed[h] + nn(qact[h], state_b[h])
         mixed[h] = value
@@ -326,26 +324,41 @@
         if (h + 1) % per == 0:
             scatter(1, h // per)
 
-    copies = [
-        store(0, normed_hbm, lambda h: mixed[h] * inv_rms * gain_ref[pl.ds(h, 1), :])
-    ]
-    for h in range(heads):
-        bscore = jnp.where(causal, nt(delta[h], vact[h]), 0.0).astype(BF16)
-        mixed[h] = (nn(bscore, kact[h]) + nt(delta[h], state_b[h])) * qslope[h]
-        dk[h] = tn(bscore, qact[h])
-        dv[h] = tn(attn[h], delta[h])
-    copies.append(store(1, qg_hbm, lambda h: mixed[h]))
+    store(normed_out, lambda h: mixed[h] * inv_rms * gain_ref[pl.ds(h, 1), :])
+
+    def local_grads(some_heads):
+        for h in some_heads:
+            bscore = jnp.where(causal, nt(delta[h], vact[h]), 0.0).astype(BF16)
+            mixed[h] = (nn(bscore, kact[h]) + nt(delta[h], state_b[h])) * qslope[h]
+            dk[h] = tn(bscore, qact[h])
+            dv[h] = tn(attn[h], delta[h])
+
+    local_grads(range(heads // 2))
+    middle(1, lambda: None)
+    local_grads(range(heads // 2, heads))
+    store(qg_out, lambda h: mixed[h])
     exchange.wait_send()
     drain(0)
 
-    middle(1)
-    for chunk in range(CHUNKS):
-        wait_back(1, chunk)
     for h in range(heads):
+        if h % per == 0:
+            wait_back(1, h // per)
         state_b[h] = scanned(1, h)
-    copies.append(store(2, kg_hbm, lambda h: (dk[h] + nt(vact[h], state_b[h])) * kslope[h]))
-    copies.append(store(3, vg_hbm, lambda h: dv[h] + nn(kact[h], state_b[h])))
+        dk[h] = (dk[h] + nt(vact[h], state_b[h])) * kslope[h]
+        dv[h] = dv[h] + nn(kact[h], state_b[h])
+    store(kg_out, lambda h: dk[h])
+    store(vg_out, lambda h: dv[h])
     drain(1)
+
+
+def deliver(*refs):
+    count = len(refs) // 2
+    sems = refs[-1]
+    copies = [
+        pltpu.make_async_copy(refs[i], refs[count + i], sems.at[i]) for i in range(count)
+    ]
+    for copy in copies:
+        copy.start()
     for copy in copies:
         copy.wait()
 
@@ -356,17 +369,16 @@
     cores = lax.axis_size("head")
     flat = (tokens * heads, width)
     rows = heads * DH // (CHUNKS * PLANE)
-    anywhere = pl.BlockSpec(memory_space=pl.ANY)
+    in_hbm = pl.BlockSpec(memory_space=pltpu.HBM)
     in_vmem = pl.BlockSpec(memory_space=pltpu.VMEM)
     per_head = (heads, GROUP, DH)
     dma = pltpu.SemaphoreType.DMA
     outs = pl.pallas_call(
         functools.partial(kernel, levels, heads, cores),
-        out_shape=[jax.ShapeDtypeStruct(flat, BF16)] * 4,
-        in_specs=[anywhere, anywhere, anywhere, in_vmem, anywhere],
-        out_specs=[anywhere] * 4,
+        out_shape=[pltpu.VMEM(flat, BF16)] * 4,
+        in_specs=[in_hbm, in_hbm, in_hbm, in_vmem, in_hbm],
+        out_specs=[in_vmem] * 4,
         scratch_shapes=[
-            pltpu.VMEM((4,) + flat, BF16),
             pltpu.VMEM((4,) + flat, BF16),
             pltpu.VMEM(per_head, BF16),
             pltpu.VMEM(per_head, BF16),
@@ -387,7 +399,6 @@
             pltpu.VMEM((2, CHUNKS, levels, rows, DH), F32),
             pltpu.VMEM((2, CHUNKS, PLANE, rows, DH), F32),
             pltpu.VMEM((2, GROUP, DH), F32),
-            dma((4,)),
             dma((4,)),
             dma((2, 2, CHUNKS)),
             dma((2, 2, CHUNKS)),
@@ -405,6 +416,14 @@
         out_gain,
         out_grad.reshape(flat),
     )
+    outs = pl.pallas_call(
+        deliver,
+        out_shape=[pltpu.HBM(flat, BF16)] * 4,
+        in_specs=[in_vmem] * 4,
+        out_specs=[in_hbm] * 4,
+        scratch_shapes=[dma((4,))],
+        compiler_params=pltpu.CompilerParams(vmem_limit_bytes=4 * 1024 * 1024),
+    )(*outs)
     return tuple(out.reshape(tokens, heads, width) for out in outs)
 
 

time: 76.8 us -> 69.3 us (0.902)
  local copies, waits for them, and re-layouts: 4.58 us -> 0 us
  Pallas kernels: 71.3 us -> 68.5 us
    unnamed x10 -> x0, local copies, waits for them, and re-layouts: 4.58 us -> none
    pallas_call x1, Pallas kernels: 71.3 us -> 67.5 us  [body(): pl.pallas_call(functools.partial(kernel, levels, heads, cores), out_shape...]
    pallas_call x0 -> x1, Pallas kernels: none -> 1 us  [body(): pl.pallas_call(deliver, out_shape=[pltpu.HBM(flat, BF16)] * 4, in_specs=[...]
where the time goes in v2:
time: 69.3 us; the launch traced here: 69.1 us
  Pallas kernels  68.5 us (99%)
    pallas_call x1, Pallas kernels, body(): pl.pallas_call(functools.partial(kernel, levels, heads, cores), out_shape...  67.5 us

profile of v2, /device:TPU:1, one launch (start us, length us, event | category | flops | bytes accessed | tf_op | source)
XLA Modules:
  0.0 69.1 jit_solution(15273945056501183870)
XLA Ops:
  0.6 67.5 %shard_map.84 = (bf16[1024,128]{1,0:T(8,128)(2,1)S(1)}, bf16[1024,128]{1,0:T(8,128)(2,1)S(1)}, bf16[1024,128]{1,0:T(8,128)(2,1)S(1)}, bf16[1024,128]{1,0:T(8,128)(2,1)S(1)}) custom-call(bf16[1024,128]{1,0:T(8,128)(2,1)} %bitcast.8, bf16[1024,128]{1,0:T(8,128)(2,1)} %bitcast.9, bf16[1024,128]{1,0:T(8,128)(2,1)} %bitcast.10, f32[4,128]{1,0:T(4,128)} %gain_ref.1, ...), custom_call_target="tpu_custom_call" | custom-call | tf_op jit(solution)/shard_map/pallas_call | solution.py:376
  68.1 1.0 %shard_map.85 = (bf16[1024,128]{1,0:T(8,128)(2,1)}, bf16[1024,128]{1,0:T(8,128)(2,1)}, bf16[1024,128]{1,0:T(8,128)(2,1)}, bf16[1024,128]{1,0:T(8,128)(2,1)}) custom-call(bf16[1024,128]{1,0:T(8,128)(2,1)S(1)} %get-tuple-element.12.refs_0_, bf16[1024,128]{1,0:T(8,128)(2,1)S(1)} %get-tuple-element.13.refs_1_, bf16[1024,128]{1,0:T(8,128)(2,1)S(1)} %get-tuple-element.14.refs_2_, ...), custom_call_target="tpu_custom_call" | custom-call | tf_op jit(solution)/shard_map/pallas_call | solution.py:419

commit v3 on v2

--- a/solution.py
+++ b/solution.py
@@ -39,13 +39,15 @@
     q_hbm,
     k_hbm,
     v_hbm,
-    gain_ref,
+    gain_hbm,
     g_hbm,
     normed_out,
     qg_out,
     kg_out,
     vg_out,
     raw,
+    results,
+    gain,
     qact,
     kact,
     vact,
@@ -71,6 +73,8 @@
     z_send_sem,
     z_recv_sem,
     stat_sem,
+    out_sem,
+    ready,
 ):
     seq = lax.axis_index("seq")
     core = lax.axis_index("head")
@@ -84,29 +88,39 @@
     def plane_peer(step):
         return lax.rem(place + step, PLANE)
 
+    loads = [
+        pltpu.make_async_copy(hbm, raw.at[i], in_sem.at[i])
+        for i, hbm in enumerate((k_hbm, v_hbm, q_hbm, g_hbm))
+    ] + [pltpu.make_async_copy(gain_hbm, gain, in_sem.at[4])]
+    for load in loads:
+        load.start()
+
     barrier = pltpu.get_barrier_semaphore()
 
     def greet_plane(step, carry):
         pl.semaphore_signal(
-            barrier, inc=1, device_id=(level * PLANE + plane_peer(step), core), device_id_type=MESH
+            barrier,
+            inc=1,
+            device_id=(level * PLANE + plane_peer(step + PLANE // 2), core),
+            device_id_type=MESH,
         )
         return carry
 
-    def greet_level(step, carry):
-        other = lax.rem(level + step, levels)
+    def greet_later(other, carry):
         pl.semaphore_signal(
             barrier, inc=1, device_id=(other * PLANE + place, core), device_id_type=MESH
         )
         return carry
 
-    loads = [
-        pltpu.make_async_copy(hbm, raw.at[i], in_sem.at[i])
-        for i, hbm in enumerate((k_hbm, v_hbm, q_hbm, g_hbm))
-    ]
-    for load in loads:
-        load.start()
-    lax.fori_loop(1, PLANE, greet_plane, 0)
-    lax.fori_loop(1, levels, greet_level, 0)
+    def answer_earlier(other, carry):
+        pl.semaphore_signal(
+            ready.at[level], inc=1, device_id=(other * PLANE + place, core), device_id_type=MESH
+        )
+        return carry
+
+    lax.fori_loop(0, PLANE // 2, greet_plane, 0)
+    lax.fori_loop(PLANE // 2 + 1, PLANE, greet_plane, 0)
+    lax.fori_loop(level + 1, levels, greet_later, 0)
     pl.semaphore_signal(barrier, inc=1, device_id=(seq, 1 - core), device_id_type=MESH)
 
     row = lax.broadcasted_iota(jnp.int32, (GROUP, GROUP), 0)
@@ -131,13 +145,16 @@
             put(act, tile, value * sigma)
             put(slope, tile, sigma * (1.0 + value * (1.0 - sigma)))
 
-    def store(out, head_value):
+    def store(i, out, head_value):
         values = [head_value(h).astype(BF16) for h in range(heads)]
         for tile in range(heads):
             piece = jnp.concatenate(
                 [value[tile * width : (tile + 1) * width] for value in values], axis=0
             )
-            out[pl.ds(tile * GROUP, GROUP), :] = nn(unsort, piece).astype(BF16)
+            results[i, pl.ds(tile * GROUP, GROUP), :] = nn(unsort, piece).astype(BF16)
+        copy = pltpu.make_async_copy(results.at[i], out, out_sem.at[i])
+        copy.start()
+        return copy
 
     def bytes_of(ref, sem):
         return pltpu.make_async_copy(ref, ref, sem)
@@ -192,6 +209,8 @@
 
             @pl.when(needed)
             def _():
+                if scan == 0 and chunk == 0:
+                    pl.semaphore_wait(ready.at[other], 1)
                 z_copy(scan, chunk, other).start()
 
     def level_prefix(scan, chunk):
@@ -267,7 +286,8 @@
     for h in range(heads):
         own[0, pl.ds(h * DH, DH), :] = tn(kact[h], vact[h])
 
-    pl.semaphore_wait(barrier, PLANE - 1 + levels - 1 + 1)
+    pl.semaphore_wait(barrier, PLANE + level)
+    lax.fori_loop(0, level, answer_earlier, 0)
     for chunk in range(CHUNKS):
         scatter(0, chunk)
 
@@ -280,10 +300,11 @@
 
     def weigh_grad():
         loads[3].wait()
+        loads[4].wait()
         for tile, value in sorted_tiles(3):
             for h in range(heads):
                 grad_in[h, pl.ds(tile * width, width), :] = (
-                    value[h * width : (h + 1) * width] * gain_ref[pl.ds(h, 1), :]
+                    value[h * width : (h + 1) * width] * gain[pl.ds(h, 1), :]
                 )
 
     middle(0, weigh_grad)
@@ -324,7 +345,7 @@
         if (h + 1) % per == 0:
             scatter(1, h // per)
 
-    store(normed_out, lambda h: mixed[h] * inv_rms * gain_ref[pl.ds(h, 1), :])
+    copies = [store(0, normed_out, lambda h: mixed[h] * inv_rms * gain[pl.ds(h, 1), :])]
 
     def local_grads(some_heads):
         for h in some_heads:
@@ -336,7 +357,7 @@
     local_grads(range(heads // 2))
     middle(1, lambda: None)
     local_grads(range(heads // 2, heads))
-    store(qg_out, lambda h: mixed[h])
+    copies.append(store(1, qg_out, lambda h: mixed[h]))
     exchange.wait_send()
     drain(0)
 
@@ -346,9 +367,11 @@
         state_b[h] = scanned(1, h)
         dk[h] = (dk[h] + nt(vact[h], state_b[h])) * kslope[h]
         dv[h] = dv[h] + nn(kact[h], state_b[h])
-    store(kg_out, lambda h: dk[h])
-    store(vg_out, lambda h: dv[h])
+    copies.append(store(2, kg_out, lambda h: dk[h]))
+    copies.append(store(3, vg_out, lambda h: dv[h]))
     drain(1)
+    for copy in copies:
+        copy.wait()
 
 
 def deliver(*refs):
@@ -369,17 +392,19 @@
     cores = lax.axis_size("head")
     flat = (tokens * heads, width)
     rows = heads * DH // (CHUNKS * PLANE)
+    anywhere = pl.BlockSpec(memory_space=pl.ANY)
     in_hbm = pl.BlockSpec(memory_space=pltpu.HBM)
-    in_vmem = pl.BlockSpec(memory_space=pltpu.VMEM)
     per_head = (heads, GROUP, DH)
     dma = pltpu.SemaphoreType.DMA
     outs = pl.pallas_call(
         functools.partial(kernel, levels, heads, cores),
         out_shape=[pltpu.VMEM(flat, BF16)] * 4,
-        in_specs=[in_hbm, in_hbm, in_hbm, in_vmem, in_hbm],
-        out_specs=[in_vmem] * 4,
+        in_specs=[in_hbm] * 5,
+        out_specs=[anywhere] * 4,
         scratch_shapes=[
             pltpu.VMEM((4,) + flat, BF16),
+            pltpu.VMEM((4,) + flat, BF16),
+            pltpu.VMEM((heads, DH), F32),
             pltpu.VMEM(per_head, BF16),
             pltpu.VMEM(per_head, BF16),
             pltpu.VMEM(per_head, BF16),
@@ -399,12 +424,14 @@
             pltpu.VMEM((2, CHUNKS, levels, rows, DH), F32),
             pltpu.VMEM((2, CHUNKS, PLANE, rows, DH), F32),
             pltpu.VMEM((2, GROUP, DH), F32),
-            dma((4,)),
+            dma((5,)),
             dma((2, 2, CHUNKS)),
             dma((2, 2, CHUNKS)),
             dma((2, CHUNKS, levels)),
             dma((2, CHUNKS, levels)),
             dma((2,)),
+            dma((4,)),
+            pltpu.SemaphoreType.REGULAR((levels,)),
         ],
         compiler_params=pltpu.CompilerParams(
             collective_id=0, has_side_effects=True, vmem_limit_bytes=60 * 1024 * 1024
@@ -419,7 +446,7 @@
     outs = pl.pallas_call(
         deliver,
         out_shape=[pltpu.HBM(flat, BF16)] * 4,
-        in_specs=[in_vmem] * 4,
+        in_specs=[anywhere] * 4,
         out_specs=[in_hbm] * 4,
         scratch_shapes=[dma((4,))],
         compiler_params=pltpu.CompilerParams(vmem_limit_bytes=4 * 1024 * 1024),

time: 69.3 us -> 66.3 us (0.957)
  Pallas kernels: 68.5 us -> 65.5 us
    pallas_call x1, Pallas kernels: 67.5 us -> 64.5 us  [body(): pl.pallas_call(functools.partial(kernel, levels, heads, cores), out_shape...]
where the time goes in v3:
time: 66.3 us; the launch traced here: 66.2 us
  Pallas kernels  65.5 us (99%)
    pallas_call x1, Pallas kernels, body(): pl.pallas_call(functools.partial(kernel, levels, heads, cores), out_shape...  64.5 us

profile of v3, /device:TPU:1, one launch (start us, length us, event | category | flops | bytes accessed | tf_op | source)
XLA Modules:
  0.0 66.2 jit_solution(13572814538879840259)
XLA Ops:
  0.6 64.5 %shard_map.84 = (bf16[1024,128]{1,0:T(8,128)(2,1)S(1)}, bf16[1024,128]{1,0:T(8,128)(2,1)S(1)}, bf16[1024,128]{1,0:T(8,128)(2,1)S(1)}, bf16[1024,128]{1,0:T(8,128)(2,1)S(1)}) custom-call(bf16[1024,128]{1,0:T(8,128)(2,1)} %bitcast.8, bf16[1024,128]{1,0:T(8,128)(2,1)} %bitcast.9, bf16[1024,128]{1,0:T(8,128)(2,1)} %bitcast.10, f32[4,128]{1,0:T(4,128)} %gain_hbm.1, ...), custom_call_target="tpu_custom_call" | custom-call | tf_op jit(solution)/shard_map/pallas_call | solution.py:399
  65.2 1.0 %shard_map.85 = (bf16[1024,128]{1,0:T(8,128)(2,1)}, bf16[1024,128]{1,0:T(8,128)(2,1)}, bf16[1024,128]{1,0:T(8,128)(2,1)}, bf16[1024,128]{1,0:T(8,128)(2,1)}) custom-call(bf16[1024,128]{1,0:T(8,128)(2,1)S(1)} %get-tuple-element.12.refs_0_, bf16[1024,128]{1,0:T(8,128)(2,1)S(1)} %get-tuple-element.13.refs_1_, bf16[1024,128]{1,0:T(8,128)(2,1)S(1)} %get-tuple-element.14.refs_2_, ...), custom_call_target="tpu_custom_call" | custom-call | tf_op jit(solution)/shard_map/pallas_call | solution.py:446

commit v4 on v3

--- a/solution.py
+++ b/solution.py
@@ -9,7 +9,8 @@
 
 GROUP = 256
 DH = 128
-PLANE = 32
+WIDE, LONG = 4, 8
+PLANE = WIDE * LONG
 CHUNKS = 2
 MESH = pl.DeviceIdType.MESH
 F32 = jnp.float32
@@ -49,6 +50,7 @@
     results,
     gain,
     qact,
+    qact_t,
     kact,
     vact,
     qslope,
@@ -85,8 +87,26 @@
     per = heads // CHUNKS
     width = GROUP // heads
 
-    def plane_peer(step):
-        return lax.rem(place + step, PLANE)
+    across, along = place // LONG, lax.rem(place, LONG)
+
+    def each_peer(act):
+        half = LONG // 2
+        steps = [half]
+        for off in range(1, half):
+            steps += [half - off, half + off]
+
+        for step in steps + [0]:
+
+            def one(turn, carry, step=step):
+                x = lax.rem(across + lax.rem(turn + WIDE // 2, WIDE), WIDE)
+                act(x * LONG + lax.rem(along + step, LONG))
+                return carry
+
+            if step:
+                lax.fori_loop(0, WIDE, one, 0)
+            else:
+                lax.fori_loop(0, WIDE // 2, one, 0)
+                lax.fori_loop(WIDE // 2 + 1, WIDE, one, 0)
 
     loads = [
         pltpu.make_async_copy(hbm, raw.at[i], in_sem.at[i])
@@ -97,14 +117,10 @@
 
     barrier = pltpu.get_barrier_semaphore()
 
-    def greet_plane(step, carry):
+    def greet(peer):
         pl.semaphore_signal(
-            barrier,
-            inc=1,
-            device_id=(level * PLANE + plane_peer(step + PLANE // 2), core),
-            device_id_type=MESH,
+            barrier, inc=1, device_id=(level * PLANE + peer, core), device_id_type=MESH
         )
-        return carry
 
     def greet_later(other, carry):
         pl.semaphore_signal(
@@ -118,8 +134,7 @@
         )
         return carry
 
-    lax.fori_loop(0, PLANE // 2, greet_plane, 0)
-    lax.fori_loop(PLANE // 2 + 1, PLANE, greet_plane, 0)
+    each_peer(greet)
     lax.fori_loop(level + 1, levels, greet_later, 0)
     pl.semaphore_signal(barrier, inc=1, device_id=(seq, 1 - core), device_id_type=MESH)
 
@@ -162,8 +177,7 @@
     others = pl.ds(0, PLANE - 1)
 
     def scatter(scan, chunk):
-        def send(step, carry):
-            peer = plane_peer(step)
+        def send(peer):
             pltpu.make_async_remote_copy(
                 src_ref=own.at[scan, pl.ds(chunk * span + peer * rows, rows), :],
                 dst_ref=gathered.at[scan, chunk, place],
@@ -172,9 +186,8 @@
                 device_id=(level * PLANE + peer, core),
                 device_id_type=MESH,
             ).start()
-            return carry
-
-        lax.fori_loop(1, PLANE, send, 0)
+
+        each_peer(send)
         gathered[scan, chunk, place] = own[scan, pl.ds(chunk * span + place * rows, rows), :]
 
     def wait_scatter(scan, chunk):
@@ -183,9 +196,8 @@
     def wait_scatter_send(scan, chunk):
         bytes_of(gathered.at[scan, chunk, others], send_sem.at[scan, 0, chunk]).wait()
 
-    def follows(scan, step):
-        other = level + step if scan == 0 else level - step
-        return (other < levels) if scan == 0 else (other >= 0), other
+    needing = ((level + 1, levels), (0, level))
+    needed = ((0, level), (level + 1, levels))
 
     def z_copy(scan, chunk, target):
         return pltpu.make_async_remote_copy(
@@ -197,46 +209,32 @@
             device_id_type=MESH,
         )
 
-    def own_prefix(scan, chunk):
-        acc = jnp.zeros((rows, DH), F32)
-        order = range(PLANE) if scan == 0 else range(PLANE - 1, -1, -1)
-        for p in order:
+    def own_total(scan, chunk):
+        acc = gathered[scan, chunk, 0]
+        for p in range(1, PLANE):
+            acc = acc + gathered[scan, chunk, p]
+        total[scan, chunk] = acc
+
+        def send(target, carry):
+            if scan == 0 and chunk == 0:
+                pl.semaphore_wait(ready.at[target], 1)
+            z_copy(scan, chunk, target).start()
+            return carry
+
+        lax.fori_loop(*needing[scan], send, 0)
+
+    def all_prefixes(scan, chunk):
+        def take(source, acc):
+            bytes_of(z_slots.at[scan, chunk, source], z_recv_sem.at[scan, chunk, source]).wait()
+            return acc + z_slots[scan, chunk, source]
+
+        acc = lax.fori_loop(*needed[scan], take, jnp.zeros((rows, DH), F32))
+        for p in range(PLANE) if scan == 0 else range(PLANE - 1, -1, -1):
             prefix[scan, chunk, p] = acc
             acc = acc + gathered[scan, chunk, p]
-        total[scan, chunk] = acc
-        for step in range(1, levels):
-            needed, other = follows(scan, step)
-
-            @pl.when(needed)
-            def _():
-                if scan == 0 and chunk == 0:
-                    pl.semaphore_wait(ready.at[other], 1)
-                z_copy(scan, chunk, other).start()
-
-    def level_prefix(scan, chunk):
-        z_slots[scan, chunk, level] = jnp.zeros((rows, DH), F32)
-        for source in range(levels):
-            earlier = source < level if scan == 0 else source > level
-
-            @pl.when(earlier)
-            def _():
-                bytes_of(
-                    z_slots.at[scan, chunk, source], z_recv_sem.at[scan, chunk, source]
-                ).wait()
-
-            @pl.when(jnp.logical_not(earlier))
-            def _():
-                z_slots[scan, chunk, source] = jnp.zeros((rows, DH), F32)
-
-        acc = jnp.zeros((rows, DH), F32)
-        for source in range(levels):
-            acc = acc + z_slots[scan, chunk, source]
-        for p in range(PLANE):
-            prefix[scan, chunk, p] = prefix[scan, chunk, p] + acc
 
     def give_back(scan, chunk):
-        def send(step, carry):
-            peer = plane_peer(step)
+        def send(peer):
             pltpu.make_async_remote_copy(
                 src_ref=prefix.at[scan, chunk, peer],
                 dst_ref=state.at[scan, chunk, place],
@@ -245,9 +243,8 @@
                 device_id=(level * PLANE + peer, core),
                 device_id_type=MESH,
             ).start()
-            return carry
-
-        lax.fori_loop(1, PLANE, send, 0)
+
+        each_peer(send)
         state[scan, chunk, place] = prefix[scan, chunk, place]
 
     def wait_back(scan, chunk):
@@ -257,20 +254,20 @@
         for chunk in range(CHUNKS):
             wait_scatter_send(scan, chunk)
             bytes_of(state.at[scan, chunk, others], send_sem.at[scan, 1, chunk]).wait()
-            for step in range(1, levels):
-                needed, other = follows(scan, step)
-
-                @pl.when(needed)
-                def _():
-                    z_copy(scan, chunk, other).wait_send()
+
+            def sent(target, carry):
+                z_copy(scan, chunk, target).wait_send()
+                return carry
+
+            lax.fori_loop(*needing[scan], sent, 0)
 
     def middle(scan, work):
         for chunk in range(CHUNKS):
             wait_scatter(scan, chunk)
-            own_prefix(scan, chunk)
+            own_total(scan, chunk)
         work()
         for chunk in range(CHUNKS):
-            level_prefix(scan, chunk)
+            all_prefixes(scan, chunk)
             give_back(scan, chunk)
 
     def scanned(scan, h):
@@ -294,6 +291,7 @@
     loads[2].wait()
     activate(2, qact, qslope)
     for h in range(heads):
+        qact_t[h] = qact[h].T
         scores = nt(qact[h], kact[h])
         attn[h] = jnp.where(causal, scores, 0.0).astype(BF16)
         mixed[h] = nn(attn[h], vact[h])
@@ -341,7 +339,7 @@
     factor = crossed * (inv_rms * inv_rms * inv_rms) * (1.0 / features)
     for h in range(heads):
         delta[h] = (grad_in[h] * inv_rms - mixed[h] * factor).astype(BF16)
-        own[1, pl.ds(h * DH, DH), :] = tn(qact[h], delta[h])
+        own[1, pl.ds(h * DH, DH), :] = nn(qact_t[h], delta[h])
         if (h + 1) % per == 0:
             scatter(1, h // per)
 
@@ -406,6 +404,7 @@
             pltpu.VMEM((4,) + flat, BF16),
             pltpu.VMEM((heads, DH), F32),
             pltpu.VMEM(per_head, BF16),
+            pltpu.VMEM((heads, DH, GROUP), BF16),
             pltpu.VMEM(per_head, BF16),
             pltpu.VMEM(per_head, BF16),
             pltpu.VMEM(per_head, F32),

time: 66.3 us -> 63.9 us (0.964)
  Pallas kernels: 65.5 us -> 63.1 us
    pallas_call x1, Pallas kernels: 64.5 us -> 62.1 us  [body(): pl.pallas_call(functools.partial(kernel, levels, heads, cores), out_shape...]
where the time goes in v4:
time: 63.9 us; the launch traced here: 63.7 us
  Pallas kernels  63.1 us (99%)
  between operations  0.64 us (1%)
    pallas_call x1, Pallas kernels, body(): pl.pallas_call(functools.partial(kernel, levels, heads, cores), out_shape...  62.1 us

profile of v4, /device:TPU:1, one launch (start us, length us, event | category | flops | bytes accessed | tf_op | source)
XLA Modules:
  0.0 63.7 jit_solution(5132563188063832166)
XLA Ops:
  0.6 62.1 %shard_map.84 = (bf16[1024,128]{1,0:T(8,128)(2,1)S(1)}, bf16[1024,128]{1,0:T(8,128)(2,1)S(1)}, bf16[1024,128]{1,0:T(8,128)(2,1)S(1)}, bf16[1024,128]{1,0:T(8,128)(2,1)S(1)}) custom-call(bf16[1024,128]{1,0:T(8,128)(2,1)} %bitcast.8, bf16[1024,128]{1,0:T(8,128)(2,1)} %bitcast.9, bf16[1024,128]{1,0:T(8,128)(2,1)} %bitcast.10, f32[4,128]{1,0:T(4,128)} %gain_hbm.1, ...), custom_call_target="tpu_custom_call" | custom-call | tf_op jit(solution)/shard_map/pallas_call | solution.py:397
  62.7 1.0 %shard_map.85 = (bf16[1024,128]{1,0:T(8,128)(2,1)}, bf16[1024,128]{1,0:T(8,128)(2,1)}, bf16[1024,128]{1,0:T(8,128)(2,1)}, bf16[1024,128]{1,0:T(8,128)(2,1)}) custom-call(bf16[1024,128]{1,0:T(8,128)(2,1)S(1)} %get-tuple-element.12.refs_0_, bf16[1024,128]{1,0:T(8,128)(2,1)S(1)} %get-tuple-element.13.refs_1_, bf16[1024,128]{1,0:T(8,128)(2,1)S(1)} %get-tuple-element.14.refs_2_, ...), custom_call_target="tpu_custom_call" | custom-call | tf_op jit(solution)/shard_map/pallas_call | solution.py:445

commit v5 on v4

--- a/solution.py
+++ b/solution.py
@@ -77,6 +77,8 @@
     stat_sem,
     out_sem,
     ready,
+    ready_plane,
+    ready_core,
 ):
     seq = lax.axis_index("seq")
     core = lax.axis_index("head")
@@ -89,6 +91,13 @@
 
     across, along = place // LONG, lax.rem(place, LONG)
 
+    def rank_of(peer):
+        x, y = peer // LONG, lax.rem(peer, LONG)
+        back = y // (LONG // 2)
+        return (y + back * (LONG + LONG // 2 - 1 - 2 * y)) * WIDE + x
+
+    rank = rank_of(place)
+
     def each_peer(act):
         half = LONG // 2
         steps = [half]
@@ -118,9 +127,11 @@
     barrier = pltpu.get_barrier_semaphore()
 
     def greet(peer):
-        pl.semaphore_signal(
-            barrier, inc=1, device_id=(level * PLANE + peer, core), device_id_type=MESH
-        )
+        @pl.when(rank_of(peer) > rank)
+        def _():
+            pl.semaphore_signal(
+                barrier, inc=1, device_id=(level * PLANE + peer, core), device_id_type=MESH
+            )
 
     def greet_later(other, carry):
         pl.semaphore_signal(
@@ -128,6 +139,16 @@
         )
         return carry
 
+    def answer(peer):
+        @pl.when(rank_of(peer) < rank)
+        def _():
+            pl.semaphore_signal(
+                ready_plane.at[place],
+                inc=1,
+                device_id=(level * PLANE + peer, core),
+                device_id_type=MESH,
+            )
+
     def answer_earlier(other, carry):
         pl.semaphore_signal(
             ready.at[level], inc=1, device_id=(other * PLANE + place, core), device_id_type=MESH
@@ -136,7 +157,10 @@
 
     each_peer(greet)
     lax.fori_loop(level + 1, levels, greet_later, 0)
-    pl.semaphore_signal(barrier, inc=1, device_id=(seq, 1 - core), device_id_type=MESH)
+
+    @pl.when(core == 0)
+    def _():
+        pl.semaphore_signal(barrier, inc=1, device_id=(seq, 1 - core), device_id_type=MESH)
 
     row = lax.broadcasted_iota(jnp.int32, (GROUP, GROUP), 0)
     col = lax.broadcasted_iota(jnp.int32, (GROUP, GROUP), 1)
@@ -176,19 +200,43 @@
 
     others = pl.ds(0, PLANE - 1)
 
+    def send_slice(scan, chunk, peer):
+        pltpu.make_async_remote_copy(
+            src_ref=own.at[scan, pl.ds(chunk * span + peer * rows, rows), :],
+            dst_ref=gathered.at[scan, chunk, place],
+            send_sem=send_sem.at[scan, 0, chunk],
+            recv_sem=recv_sem.at[scan, 0, chunk],
+            device_id=(level * PLANE + peer, core),
+            device_id_type=MESH,
+        ).start()
+
+    def keep_slice(scan, chunk):
+        gathered[scan, chunk, place] = own[scan, pl.ds(chunk * span + place * rows, rows), :]
+
     def scatter(scan, chunk):
-        def send(peer):
-            pltpu.make_async_remote_copy(
-                src_ref=own.at[scan, pl.ds(chunk * span + peer * rows, rows), :],
-                dst_ref=gathered.at[scan, chunk, place],
-                send_sem=send_sem.at[scan, 0, chunk],
-                recv_sem=recv_sem.at[scan, 0, chunk],
-                device_id=(level * PLANE + peer, core),
-                device_id_type=MESH,
-            ).start()
-
-        each_peer(send)
-        gathered[scan, chunk, place] = own[scan, pl.ds(chunk * span + place * rows, rows), :]
+        each_peer(lambda peer: send_slice(scan, chunk, peer))
+        keep_slice(scan, chunk)
+
+    def first_scatter():
+        for chunk in range(CHUNKS):
+
+            def to_earlier(peer):
+                @pl.when(rank_of(peer) < rank)
+                def _():
+                    send_slice(0, chunk, peer)
+
+            each_peer(to_earlier)
+
+        def to_later(peer):
+            @pl.when(rank_of(peer) > rank)
+            def _():
+                pl.semaphore_wait(ready_plane.at[peer], 1)
+                for chunk in range(CHUNKS):
+                    send_slice(0, chunk, peer)
+
+        each_peer(to_later)
+        for chunk in range(CHUNKS):
+            keep_slice(0, chunk)
 
     def wait_scatter(scan, chunk):
         bytes_of(gathered.at[scan, chunk, others], recv_sem.at[scan, 0, chunk]).wait()
@@ -283,10 +331,20 @@
     for h in range(heads):
         own[0, pl.ds(h * DH, DH), :] = tn(kact[h], vact[h])
 
-    pl.semaphore_wait(barrier, PLANE + level)
+    earlier = rank + level + core
+
+    @pl.when(earlier > 0)
+    def _():
+        pl.semaphore_wait(barrier, earlier)
+
     lax.fori_loop(0, level, answer_earlier, 0)
-    for chunk in range(CHUNKS):
-        scatter(0, chunk)
+    each_peer(answer)
+
+    @pl.when(core == 1)
+    def _():
+        pl.semaphore_signal(ready_core, inc=1, device_id=(seq, 1 - core), device_id_type=MESH)
+
+    first_scatter()
 
     loads[2].wait()
     activate(2, qact, qslope)
@@ -329,6 +387,11 @@
         device_id=(seq, 1 - core),
         device_id_type=MESH,
     )
+
+    @pl.when(core == 0)
+    def _():
+        pl.semaphore_wait(ready_core, 1)
+
     exchange.start()
     exchange.wait_recv()
     both = stats[1]
@@ -431,6 +494,8 @@
             dma((2,)),
             dma((4,)),
             pltpu.SemaphoreType.REGULAR((levels,)),
+            pltpu.SemaphoreType.REGULAR((PLANE,)),
+            pltpu.SemaphoreType.REGULAR,
         ],
         compiler_params=pltpu.CompilerParams(
             collective_id=0, has_side_effects=True, vmem_limit_bytes=60 * 1024 * 1024

time: 63.9 us -> 69.3 us (1.085)
  Pallas kernels: 63.1 us -> 68.5 us
    pallas_call x1, Pallas kernels: 62.1 us -> 67.5 us  [body(): pl.pallas_call(functools.partial(kernel, levels, heads, cores), out_shape...]
where the time goes in v5:
time: 69.3 us; the launch traced here: 69.1 us
  Pallas kernels  68.5 us (99%)
    pallas_call x1, Pallas kernels, body(): pl.pallas_call(functools.partial(kernel, levels, heads, cores), out_shape...  67.5 us

profile of v5, /device:TPU:1, one launch (start us, length us, event | category | flops | bytes accessed | tf_op | source)
XLA Modules:
  0.0 69.1 jit_solution(3839700125511744294)
XLA Ops:
  0.6 67.5 %shard_map.84 = (bf16[1024,128]{1,0:T(8,128)(2,1)S(1)}, bf16[1024,128]{1,0:T(8,128)(2,1)S(1)}, bf16[1024,128]{1,0:T(8,128)(2,1)S(1)}, bf16[1024,128]{1,0:T(8,128)(2,1)S(1)}) custom-call(bf16[1024,128]{1,0:T(8,128)(2,1)} %bitcast.8, bf16[1024,128]{1,0:T(8,128)(2,1)} %bitcast.9, bf16[1024,128]{1,0:T(8,128)(2,1)} %bitcast.10, f32[4,128]{1,0:T(4,128)} %gain_hbm.1, ...), custom_call_target="tpu_custom_call" | custom-call | tf_op jit(solution)/shard_map/pallas_call | solution.py:460
  68.1 1.0 %shard_map.85 = (bf16[1024,128]{1,0:T(8,128)(2,1)}, bf16[1024,128]{1,0:T(8,128)(2,1)}, bf16[1024,128]{1,0:T(8,128)(2,1)}, bf16[1024,128]{1,0:T(8,128)(2,1)}) custom-call(bf16[1024,128]{1,0:T(8,128)(2,1)S(1)} %get-tuple-element.12.refs_0_, bf16[1024,128]{1,0:T(8,128)(2,1)S(1)} %get-tuple-element.13.refs_1_, bf16[1024,128]{1,0:T(8,128)(2,1)S(1)} %get-tuple-element.14.refs_2_, ...), custom_call_target="tpu_custom_call" | custom-call | tf_op jit(solution)/shard_map/pallas_call | solution.py:510

commit v6 on v4

--- a/solution.py
+++ b/solution.py
@@ -108,33 +108,32 @@
                 lax.fori_loop(0, WIDE // 2, one, 0)
                 lax.fori_loop(WIDE // 2 + 1, WIDE, one, 0)
 
+    barrier = pltpu.get_barrier_semaphore()
+
+    def greet(peer):
+        pl.semaphore_signal(
+            barrier, inc=1, device_id=(level * PLANE + peer, core), device_id_type=MESH
+        )
+
+    def greet_later(other, carry):
+        pl.semaphore_signal(
+            barrier, inc=1, device_id=(other * PLANE + place, core), device_id_type=MESH
+        )
+        return carry
+
+    def answer_earlier(other, carry):
+        pl.semaphore_signal(
+            ready.at[level], inc=1, device_id=(other * PLANE + place, core), device_id_type=MESH
+        )
+        return carry
+
+    each_peer(greet)
     loads = [
         pltpu.make_async_copy(hbm, raw.at[i], in_sem.at[i])
         for i, hbm in enumerate((k_hbm, v_hbm, q_hbm, g_hbm))
     ] + [pltpu.make_async_copy(gain_hbm, gain, in_sem.at[4])]
     for load in loads:
         load.start()
-
-    barrier = pltpu.get_barrier_semaphore()
-
-    def greet(peer):
-        pl.semaphore_signal(
-            barrier, inc=1, device_id=(level * PLANE + peer, core), device_id_type=MESH
-        )
-
-    def greet_later(other, carry):
-        pl.semaphore_signal(
-            barrier, inc=1, device_id=(other * PLANE + place, core), device_id_type=MESH
-        )
-        return carry
-
-    def answer_earlier(other, carry):
-        pl.semaphore_signal(
-            ready.at[level], inc=1, device_id=(other * PLANE + place, core), device_id_type=MESH
-        )
-        return carry
-
-    each_peer(greet)
     lax.fori_loop(level + 1, levels, greet_later, 0)
     pl.semaphore_signal(barrier, inc=1, device_id=(seq, 1 - core), device_id_type=MESH)
 
@@ -244,7 +243,20 @@
                 device_id_type=MESH,
             ).start()
 
-        each_peer(send)
+        if scan == 0:
+            each_peer(send)
+        else:
+
+            @pl.when(place != 0)
+            def _():
+                send(0)
+
+            def unless_first(peer):
+                @pl.when(peer != 0)
+                def _():
+                    send(peer)
+
+            each_peer(unless_first)
         state[scan, chunk, place] = prefix[scan, chunk, place]
 
     def wait_back(scan, chunk):

time: 63.9 us -> 62.5 us (0.978)
  Pallas kernels: 63.1 us -> 61.7 us
    pallas_call x1, Pallas kernels: 62.1 us -> 60.7 us  [body(): pl.pallas_call(functools.partial(kernel, levels, heads, cores), out_shape...]
where the time goes in v6:
time: 62.5 us; the launch traced here: 62.4 us
  Pallas kernels  61.7 us (99%)
  between operations  0.64 us (1%)
    pallas_call x1, Pallas kernels, body(): pl.pallas_call(functools.partial(kernel, levels, heads, cores), out_shape...  60.7 us

profile of v6, /device:TPU:1, one launch (start us, length us, event | category | flops | bytes accessed | tf_op | source)
XLA Modules:
  0.0 62.4 jit_solution(3473812847196159670)
XLA Ops:
  0.6 60.7 %shard_map.84 = (bf16[1024,128]{1,0:T(8,128)(2,1)S(1)}, bf16[1024,128]{1,0:T(8,128)(2,1)S(1)}, bf16[1024,128]{1,0:T(8,128)(2,1)S(1)}, bf16[1024,128]{1,0:T(8,128)(2,1)S(1)}) custom-call(bf16[1024,128]{1,0:T(8,128)(2,1)} %bitcast.8, bf16[1024,128]{1,0:T(8,128)(2,1)} %bitcast.9, bf16[1024,128]{1,0:T(8,128)(2,1)} %bitcast.10, f32[4,128]{1,0:T(4,128)} %gain_hbm.1, ...), custom_call_target="tpu_custom_call" | custom-call | tf_op jit(solution)/shard_map/pallas_call | solution.py:409
  61.4 1.0 %shard_map.85 = (bf16[1024,128]{1,0:T(8,128)(2,1)}, bf16[1024,128]{1,0:T(8,128)(2,1)}, bf16[1024,128]{1,0:T(8,128)(2,1)}, bf16[1024,128]{1,0:T(8,128)(2,1)}) custom-call(bf16[1024,128]{1,0:T(8,128)(2,1)S(1)} %get-tuple-element.12.refs_0_, bf16[1024,128]{1,0:T(8,128)(2,1)S(1)} %get-tuple-element.13.refs_1_, bf16[1024,128]{1,0:T(8,128)(2,1)S(1)} %get-tuple-element.14.refs_2_, ...), custom_call_target="tpu_custom_call" | custom-call | tf_op jit(solution)/shard_map/pallas_call | solution.py:457

commit v7 on v6

--- a/solution.py
+++ b/solution.py
@@ -11,6 +11,7 @@
 DH = 128
 WIDE, LONG = 4, 8
 PLANE = WIDE * LONG
+RELAY = 3
 CHUNKS = 2
 MESH = pl.DeviceIdType.MESH
 F32 = jnp.float32
@@ -77,6 +78,7 @@
     stat_sem,
     out_sem,
     ready,
+    relay_sem,
 ):
     seq = lax.axis_index("seq")
     core = lax.axis_index("head")
@@ -217,17 +219,50 @@
         def send(target, carry):
             if scan == 0 and chunk == 0:
                 pl.semaphore_wait(ready.at[target], 1)
-            z_copy(scan, chunk, target).start()
+            if scan == 0:
+
+                @pl.when(target - level != 2 * RELAY)
+                def _():
+                    z_copy(scan, chunk, target).start()
+            else:
+                z_copy(scan, chunk, target).start()
             return carry
 
         lax.fori_loop(*needing[scan], send, 0)
+
+    relays = jnp.logical_and(level >= RELAY, level + RELAY < levels)
+
+    def relay_copy(chunk):
+        slot = lax.rem(level + levels - RELAY, levels)
+        target = lax.rem(level + RELAY, levels)
+        return pltpu.make_async_remote_copy(
+            src_ref=z_slots.at[0, chunk, slot],
+            dst_ref=z_slots.at[0, chunk, slot],
+            send_sem=relay_sem.at[chunk],
+            recv_sem=z_recv_sem.at[0, chunk, slot],
+            device_id=(target * PLANE + place, core),
+            device_id_type=MESH,
+        )
+
+    def pass_on(chunk):
+        @pl.when(relays)
+        def _():
+            relay_copy(chunk).start()
 
     def all_prefixes(scan, chunk):
         def take(source, acc):
             bytes_of(z_slots.at[scan, chunk, source], z_recv_sem.at[scan, chunk, source]).wait()
             return acc + z_slots[scan, chunk, source]
 
-        acc = lax.fori_loop(*needed[scan], take, jnp.zeros((rows, DH), F32))
+        acc = jnp.zeros((rows, DH), F32)
+        if scan == 0:
+            middle = jnp.maximum(level - RELAY, 0)
+            acc = lax.fori_loop(middle, jnp.minimum(middle + 1, level), take, acc)
+            pass_on(chunk)
+            acc = lax.fori_loop(0, middle, take, acc)
+            acc = lax.fori_loop(middle + 1, level, take, acc)
+        else:
+            acc = lax.fori_loop(*needed[scan], take, acc)
         for p in range(PLANE) if scan == 0 else range(PLANE - 1, -1, -1):
             prefix[scan, chunk, p] = acc
             acc = acc + gathered[scan, chunk, p]
@@ -268,10 +303,21 @@
             bytes_of(state.at[scan, chunk, others], send_sem.at[scan, 1, chunk]).wait()
 
             def sent(target, carry):
-                z_copy(scan, chunk, target).wait_send()
+                if scan == 0:
+
+                    @pl.when(target - level != 2 * RELAY)
+                    def _():
+                        z_copy(scan, chunk, target).wait_send()
+                else:
+                    z_copy(scan, chunk, target).wait_send()
                 return carry
 
             lax.fori_loop(*needing[scan], sent, 0)
+            if scan == 0:
+
+                @pl.when(relays)
+                def _():
+                    relay_copy(chunk).wait_send()
 
     def middle(scan, work):
         for chunk in range(CHUNKS):
@@ -443,6 +489,7 @@
             dma((2,)),
             dma((4,)),
             pltpu.SemaphoreType.REGULAR((levels,)),
+            dma((CHUNKS,)),
         ],
         compiler_params=pltpu.CompilerParams(
             collective_id=0, has_side_effects=True, vmem_limit_bytes=60 * 1024 * 1024

time: 62.5 us -> 63.7 us (1.019)
  Pallas kernels: 61.7 us -> 62.8 us
    pallas_call x1, Pallas kernels: 60.7 us -> 61.8 us  [body(): pl.pallas_call(functools.partial(kernel, levels, heads, cores), out_shape...]
where the time goes in v7:
time: 63.7 us; the launch traced here: 63.4 us
  Pallas kernels  62.8 us (99%)
  between operations  0.64 us (1%)
    pallas_call x1, Pallas kernels, body(): pl.pallas_call(functools.partial(kernel, levels, heads, cores), out_shape...  61.8 us

profile of v7, /device:TPU:1, one launch (start us, length us, event | category | flops | bytes accessed | tf_op | source)
XLA Modules:
  0.0 63.4 jit_solution(11533702496891335821)
XLA Ops:
  0.6 61.8 %shard_map.84 = (bf16[1024,128]{1,0:T(8,128)(2,1)S(1)}, bf16[1024,128]{1,0:T(8,128)(2,1)S(1)}, bf16[1024,128]{1,0:T(8,128)(2,1)S(1)}, bf16[1024,128]{1,0:T(8,128)(2,1)S(1)}) custom-call(bf16[1024,128]{1,0:T(8,128)(2,1)} %bitcast.8, bf16[1024,128]{1,0:T(8,128)(2,1)} %bitcast.9, bf16[1024,128]{1,0:T(8,128)(2,1)} %bitcast.10, f32[4,128]{1,0:T(4,128)} %gain_hbm.1, ...), custom_call_target="tpu_custom_call" | custom-call | tf_op jit(solution)/shard_map/pallas_call | solution.py:455
  62.4 1.0 %shard_map.85 = (bf16[1024,128]{1,0:T(8,128)(2,1)}, bf16[1024,128]{1,0:T(8,128)(2,1)}, bf16[1024,128]{1,0:T(8,128)(2,1)}, bf16[1024,128]{1,0:T(8,128)(2,1)}) custom-call(bf16[1024,128]{1,0:T(8,128)(2,1)S(1)} %get-tuple-element.12.refs_0_, bf16[1024,128]{1,0:T(8,128)(2,1)S(1)} %get-tuple-element.13.refs_1_, bf16[1024,128]{1,0:T(8,128)(2,1)S(1)} %get-tuple-element.14.refs_2_, ...), custom_call_target="tpu_custom_call" | custom-call | tf_op jit(solution)/shard_map/pallas_call | solution.py:504

commit v8 on v6

--- a/solution.py
+++ b/solution.py
@@ -11,7 +11,7 @@
 DH = 128
 WIDE, LONG = 4, 8
 PLANE = WIDE * LONG
-CHUNKS = 2
+CHUNKS = (1, 2)
 MESH = pl.DeviceIdType.MESH
 F32 = jnp.float32
 BF16 = jnp.bfloat16
@@ -82,9 +82,9 @@
     core = lax.axis_index("head")
     level = seq // PLANE
     place = lax.rem(seq, PLANE)
-    rows = heads * DH // (CHUNKS * PLANE)
-    span = heads * DH // CHUNKS
-    per = heads // CHUNKS
+    rows = [heads * DH // (count * PLANE) for count in CHUNKS]
+    span = [heads * DH // count for count in CHUNKS]
+    per = [heads // count for count in CHUNKS]
     width = GROUP // heads
 
     across, along = place // LONG, lax.rem(place, LONG)
@@ -178,8 +178,8 @@
     def scatter(scan, chunk):
         def send(peer):
             pltpu.make_async_remote_copy(
-                src_ref=own.at[scan, pl.ds(chunk * span + peer * rows, rows), :],
-                dst_ref=gathered.at[scan, chunk, place],
+                src_ref=own.at[scan, pl.ds(chunk * span[scan] + peer * rows[scan], rows[scan]), :],
+                dst_ref=gathered[scan].at[chunk, place],
                 send_sem=send_sem.at[scan, 0, chunk],
                 recv_sem=recv_sem.at[scan, 0, chunk],
                 device_id=(level * PLANE + peer, core),
@@ -187,21 +187,23 @@
             ).start()
 
         each_peer(send)
-        gathered[scan, chunk, place] = own[scan, pl.ds(chunk * span + place * rows, rows), :]
+        gathered[scan][chunk, place] = own[
+            scan, pl.ds(chunk * span[scan] + place * rows[scan], rows[scan]), :
+        ]
 
     def wait_scatter(scan, chunk):
-        bytes_of(gathered.at[scan, chunk, others], recv_sem.at[scan, 0, chunk]).wait()
+        bytes_of(gathered[scan].at[chunk, others], recv_sem.at[scan, 0, chunk]).wait()
 
     def wait_scatter_send(scan, chunk):
-        bytes_of(gathered.at[scan, chunk, others], send_sem.at[scan, 0, chunk]).wait()
+        bytes_of(gathered[scan].at[chunk, others], send_sem.at[scan, 0, chunk]).wait()
 
     needing = ((level + 1, levels), (0, level))
     needed = ((0, level), (level + 1, levels))
 
     def z_copy(scan, chunk, target):
         return pltpu.make_async_remote_copy(
-            src_ref=total.at[scan, chunk],
-            dst_ref=z_slots.at[scan, chunk, level],
+            src_ref=total[scan].at[chunk],
+            dst_ref=z_slots[scan].at[chunk, level],
             send_sem=z_send_sem.at[scan, chunk, target],
             recv_sem=z_recv_sem.at[scan, chunk, level],
             device_id=(target * PLANE + place, core),
@@ -209,10 +211,10 @@
         )
 
     def own_total(scan, chunk):
-        acc = gathered[scan, chunk, 0]
+        acc = gathered[scan][chunk, 0]
         for p in range(1, PLANE):
-            acc = acc + gathered[scan, chunk, p]
-        total[scan, chunk] = acc
+            acc = acc + gathered[scan][chunk, p]
+        total[scan][chunk] = acc
 
         def send(target, carry):
             if scan == 0 and chunk == 0:
@@ -224,19 +226,19 @@
 
     def all_prefixes(scan, chunk):
         def take(source, acc):
-            bytes_of(z_slots.at[scan, chunk, source], z_recv_sem.at[scan, chunk, source]).wait()
-            return acc + z_slots[scan, chunk, source]
-
-        acc = lax.fori_loop(*needed[scan], take, jnp.zeros((rows, DH), F32))
+            bytes_of(z_slots[scan].at[chunk, source], z_recv_sem.at[scan, chunk, source]).wait()
+            return acc + z_slots[scan][chunk, source]
+
+        acc = lax.fori_loop(*needed[scan], take, jnp.zeros((rows[scan], DH), F32))
         for p in range(PLANE) if scan == 0 else range(PLANE - 1, -1, -1):
-            prefix[scan, chunk, p] = acc
-            acc = acc + gathered[scan, chunk, p]
+            prefix[scan][chunk, p] = acc
+            acc = acc + gathered[scan][chunk, p]
 
     def give_back(scan, chunk):
         def send(peer):
             pltpu.make_async_remote_copy(
-                src_ref=prefix.at[scan, chunk, peer],
-                dst_ref=state.at[scan, chunk, place],
+                src_ref=prefix[scan].at[chunk, peer],
+                dst_ref=state[scan].at[chunk, place],
                 send_sem=send_sem.at[scan, 1, chunk],
                 recv_sem=recv_sem.at[scan, 1, chunk],
                 device_id=(level * PLANE + peer, core),
@@ -257,15 +259,15 @@
                     send(peer)
 
             each_peer(unless_first)
-        state[scan, chunk, place] = prefix[scan, chunk, place]
+        state[scan][chunk, place] = prefix[scan][chunk, place]
 
     def wait_back(scan, chunk):
-        bytes_of(state.at[scan, chunk, others], recv_sem.at[scan, 1, chunk]).wait()
+        bytes_of(state[scan].at[chunk, others], recv_sem.at[scan, 1, chunk]).wait()
 
     def drain(scan):
-        for chunk in range(CHUNKS):
+        for chunk in range(CHUNKS[scan]):
             wait_scatter_send(scan, chunk)
-            bytes_of(state.at[scan, chunk, others], send_sem.at[scan, 1, chunk]).wait()
+            bytes_of(state[scan].at[chunk, others], send_sem.at[scan, 1, chunk]).wait()
 
             def sent(target, carry):
                 z_copy(scan, chunk, target).wait_send()
@@ -274,18 +276,18 @@
             lax.fori_loop(*needing[scan], sent, 0)
 
     def middle(scan, work):
-        for chunk in range(CHUNKS):
+        for chunk in range(CHUNKS[scan]):
             wait_scatter(scan, chunk)
             own_total(scan, chunk)
         work()
-        for chunk in range(CHUNKS):
+        for chunk in range(CHUNKS[scan]):
             all_prefixes(scan, chunk)
             give_back(scan, chunk)
 
     def scanned(scan, h):
-        chunk, at = h // per, h % per
-        parts = PLANE // per
-        return state[scan, chunk, pl.ds(at * parts, parts)].reshape(DH, DH).astype(BF16)
+        chunk, at = h // per[scan], h % per[scan]
+        parts = PLANE // per[scan]
+        return state[scan][chunk, pl.ds(at * parts, parts)].reshape(DH, DH).astype(BF16)
 
     loads[0].wait()
     activate(0, kact, kslope)
@@ -297,7 +299,7 @@
 
     pl.semaphore_wait(barrier, PLANE + level)
     lax.fori_loop(0, level, answer_earlier, 0)
-    for chunk in range(CHUNKS):
+    for chunk in range(CHUNKS[0]):
         scatter(0, chunk)
 
     loads[2].wait()
@@ -322,8 +324,8 @@
     square = jnp.zeros((GROUP, DH), F32)
     crossed = jnp.zeros((GROUP, DH), F32)
     for h in range(heads):
-        if h % per == 0:
-            wait_back(0, h // per)
+        if h % per[0] == 0:
+            wait_back(0, h // per[0])
         state_b[h] = scanned(0, h)
         value = mixed[h] + nn(qact[h], state_b[h])
         mixed[h] = value
@@ -352,8 +354,8 @@
     for h in range(heads):
         delta[h] = (grad_in[h] * inv_rms - mixed[h] * factor).astype(BF16)
         own[1, pl.ds(h * DH, DH), :] = nn(qact_t[h], delta[h])
-        if (h + 1) % per == 0:
-            scatter(1, h // per)
+        if (h + 1) % per[1] == 0:
+            scatter(1, h // per[1])
 
     copies = [store(0, normed_out, lambda h: mixed[h] * inv_rms * gain[pl.ds(h, 1), :])]
 
@@ -372,8 +374,8 @@
     drain(0)
 
     for h in range(heads):
-        if h % per == 0:
-            wait_back(1, h // per)
+        if h % per[1] == 0:
+            wait_back(1, h // per[1])
         state_b[h] = scanned(1, h)
         dk[h] = (dk[h] + nt(vact[h], state_b[h])) * kslope[h]
         dv[h] = dv[h] + nn(kact[h], state_b[h])
@@ -401,7 +403,14 @@
     levels = lax.axis_size("seq") // PLANE
     cores = lax.axis_size("head")
     flat = (tokens * heads, width)
-    rows = heads * DH // (CHUNKS * PLANE)
+    most = max(CHUNKS)
+
+    def per_scan(*slots):
+        return [
+            pltpu.VMEM((count,) + slots + (heads * DH // (count * PLANE), DH), F32)
+            for count in CHUNKS
+        ]
+
     anywhere = pl.BlockSpec(memory_space=pl.ANY)
     in_hbm = pl.BlockSpec(memory_space=pltpu.HBM)
     per_head = (heads, GROUP, DH)
@@ -429,17 +438,17 @@
             pltpu.VMEM(per_head, F32),
             pltpu.VMEM((heads, DH, DH), BF16),
             pltpu.VMEM((2, heads * DH, DH), F32),
-            pltpu.VMEM((2, CHUNKS, PLANE, rows, DH), F32),
-            pltpu.VMEM((2, CHUNKS, PLANE, rows, DH), F32),
-            pltpu.VMEM((2, CHUNKS, rows, DH), F32),
-            pltpu.VMEM((2, CHUNKS, levels, rows, DH), F32),
-            pltpu.VMEM((2, CHUNKS, PLANE, rows, DH), F32),
+            per_scan(PLANE),
+            per_scan(PLANE),
+            per_scan(),
+            per_scan(levels),
+            per_scan(PLANE),
             pltpu.VMEM((2, GROUP, DH), F32),
             dma((5,)),
-            dma((2, 2, CHUNKS)),
-            dma((2, 2, CHUNKS)),
-            dma((2, CHUNKS, levels)),
-            dma((2, CHUNKS, levels)),
+            dma((2, 2, most)),
+            dma((2, 2, most)),
+            dma((2, most, levels)),
+            dma((2, most, levels)),
             dma((2,)),
             dma((4,)),
             pltpu.SemaphoreType.REGULAR((levels,)),

time: 62.5 us -> 64.3 us (1.029)
  Pallas kernels: 61.7 us -> 62.9 us
    pallas_call x1, Pallas kernels: 60.7 us -> 61.9 us  [body(): pl.pallas_call(functools.partial(kernel, levels, heads, cores), out_shape...]
where the time goes in v8:
time: 64.3 us; the launch traced here: 63.6 us
  Pallas kernels  62.9 us (98%)
    pallas_call x1, Pallas kernels, body(): pl.pallas_call(functools.partial(kernel, levels, heads, cores), out_shape...  61.9 us

profile of v8, /device:TPU:1, one launch (start us, length us, event | category | flops | bytes accessed | tf_op | source)
XLA Modules:
  0.0 63.6 jit_solution(9353186873082958272)
XLA Ops:
  0.6 61.9 %shard_map.84 = (bf16[1024,128]{1,0:T(8,128)(2,1)S(1)}, bf16[1024,128]{1,0:T(8,128)(2,1)S(1)}, bf16[1024,128]{1,0:T(8,128)(2,1)S(1)}, bf16[1024,128]{1,0:T(8,128)(2,1)S(1)}) custom-call(bf16[1024,128]{1,0:T(8,128)(2,1)} %bitcast.8, bf16[1024,128]{1,0:T(8,128)(2,1)} %bitcast.9, bf16[1024,128]{1,0:T(8,128)(2,1)} %bitcast.10, f32[4,128]{1,0:T(4,128)} %gain_hbm.1, ...), custom_call_target="tpu_custom_call" | custom-call | tf_op jit(solution)/shard_map/pallas_call | solution.py:418
  62.6 1.0 %shard_map.85 = (bf16[1024,128]{1,0:T(8,128)(2,1)}, bf16[1024,128]{1,0:T(8,128)(2,1)}, bf16[1024,128]{1,0:T(8,128)(2,1)}, bf16[1024,128]{1,0:T(8,128)(2,1)}) custom-call(bf16[1024,128]{1,0:T(8,128)(2,1)S(1)} %get-tuple-element.12.refs_0_, bf16[1024,128]{1,0:T(8,128)(2,1)S(1)} %get-tuple-element.13.refs_1_, bf16[1024,128]{1,0:T(8,128)(2,1)S(1)} %get-tuple-element.14.refs_2_, ...), custom_call_target="tpu_custom_call" | custom-call | tf_op jit(solution)/shard_map/pallas_call | solution.py:466

commit v9 on v6

--- a/solution.py
+++ b/solution.py
@@ -317,7 +317,8 @@
                     value[h * width : (h + 1) * width] * gain[pl.ds(h, 1), :]
                 )
 
-    middle(0, weigh_grad)
+    weigh_grad()
+    middle(0, lambda: None)
 
     square = jnp.zeros((GROUP, DH), F32)
     crossed = jnp.zeros((GROUP, DH), F32)

time: 62.5 us -> 62.7 us (level)
  no operation moved by 1% of the time
where the time goes in v9:
time: 62.7 us; the launch traced here: 62.3 us
  Pallas kernels  61.6 us (98%)
  between operations  0.64 us (1%)
    pallas_call x1, Pallas kernels, body(): pl.pallas_call(functools.partial(kernel, levels, heads, cores), out_shape...  60.6 us

profile of v9, /device:TPU:1, one launch (start us, length us, event | category | flops | bytes accessed | tf_op | source)
XLA Modules:
  0.0 62.3 jit_solution(8695396109461232938)
XLA Ops:
  0.6 60.6 %shard_map.84 = (bf16[1024,128]{1,0:T(8,128)(2,1)S(1)}, bf16[1024,128]{1,0:T(8,128)(2,1)S(1)}, bf16[1024,128]{1,0:T(8,128)(2,1)S(1)}, bf16[1024,128]{1,0:T(8,128)(2,1)S(1)}) custom-call(bf16[1024,128]{1,0:T(8,128)(2,1)} %bitcast.8, bf16[1024,128]{1,0:T(8,128)(2,1)} %bitcast.9, bf16[1024,128]{1,0:T(8,128)(2,1)} %bitcast.10, f32[4,128]{1,0:T(4,128)} %gain_hbm.1, ...), custom_call_target="tpu_custom_call" | custom-call | tf_op jit(solution)/shard_map/pallas_call | solution.py:410
  61.3 1.0 %shard_map.85 = (bf16[1024,128]{1,0:T(8,128)(2,1)}, bf16[1024,128]{1,0:T(8,128)(2,1)}, bf16[1024,128]{1,0:T(8,128)(2,1)}, bf16[1024,128]{1,0:T(8,128)(2,1)}) custom-call(bf16[1024,128]{1,0:T(8,128)(2,1)S(1)} %get-tuple-element.12.refs_0_, bf16[1024,128]{1,0:T(8,128)(2,1)S(1)} %get-tuple-element.13.refs_1_, bf16[1024,128]{1,0:T(8,128)(2,1)S(1)} %get-tuple-element.14.refs_2_, ...), custom_call_target="tpu_custom_call" | custom-call | tf_op jit(solution)/shard_map/pallas_call | solution.py:458
